TPU v7x, 512 devices: a whole 4x4x16 slice. The times are simulated.
512 devices in a mesh: mem: 8 (over z_hi, x), tile: 64 (over y, z_lo, core).
Axes of the slice: x: 4, y: 4, z: 16 (z_hi: 2, z_lo: 8; z = z_hi * 8 + z_lo), core: 2. Of those that a mesh axis runs over, the one named last changes fastest.
Arguments:
- vector: float32 [2, 64, 64, 256], P(None, 'tile'), may hold values from -6 to 6
- ensemble: bfloat16 [16, 2, 64, 64, 256], P('mem', None, 'tile'), may hold values from -6 to 6
- diffusivity: float32 [2, 64, 64, 256], P(None, 'tile'), may hold values from 0.04 to 0.24
- norm_weight: float32 [64, 64, 256], P('tile'), may hold values from 0.5 to 2
- static_var: float32 [2, 64, 64, 256], P(None, 'tile'), may hold values from 0.2 to 2
Outputs:
- increment: float32 [2, 64, 64, 256], P(None, 'tile')
All inputs are finite; a program needn't handle non-finite values.
Results may differ from a plain program's by a relative error of at most 0.0003.
Values sent between devices are 32-bit elements; how exact they have to be, the bound alone decides.
No kernel may reach another device: no remote copies, remote signals or barrier semaphores. Data moves between devices by JAX's collectives and lax.ppermute only.
A program may use at most 64 MiB of HBM per device.

v0:
```python
import jax
import jax.numpy as jnp
from jax import lax
from jax.sharding import PartitionSpec as P

COL_TILES = 8
SWEEPS = 8
HALO = 3


ens_weight = 0.7
static_weight = 0.3


def passed_along(block, axis, distance):
    devices = range(lax.axis_size(axis))
    route = [(i - distance, i) for i in devices if i - distance in devices]
    return lax.ppermute(block, axis, route)


def diffuse(values, row_coef, col_coef):
    row_flux = row_coef[:-1, 1:-1] * (values[..., 1:, 1:-1] - values[..., :-1, 1:-1])
    col_flux = col_coef[1:-1, :-1] * (values[..., 1:-1, 1:] - values[..., 1:-1, :-1])
    return (
        values[..., 1:-1, 1:-1]
        + row_flux[..., 1:, :]
        - row_flux[..., :-1, :]
        + col_flux[..., 1:]
        - col_flux[..., :-1]
    )


def margin(field, depth):
    above = passed_along(field[..., -depth:, :], "tile", COL_TILES)
    below = passed_along(field[..., :depth, :], "tile", -COL_TILES)
    tall = jnp.concatenate([above, field, below], -2)
    left = passed_along(tall[..., -depth:], "tile", 1)
    right = passed_along(tall[..., :depth], "tile", -1)
    col_block = lax.axis_index("tile") % COL_TILES
    left = jnp.where(col_block == 0, jnp.float32(0.0), left)
    right = jnp.where(col_block == COL_TILES - 1, jnp.float32(0.0), right)
    return jnp.concatenate([left, tall, right], -1)


def local(vector, ensemble, diffusivity, norm_weight, static_var):
    vec = vector[:, 0]
    weight = norm_weight[0]
    nrows = vec.shape[1]
    ncols = vec.shape[2]
    tile_id = lax.axis_index("tile")
    row_block = tile_id // COL_TILES
    col_block = tile_id % COL_TILES
    total_rows = lax.axis_size("tile") // COL_TILES * nrows
    total_cols = COL_TILES * ncols
    global_row = row_block * nrows + jnp.arange(nrows)[:, None]
    global_col = col_block * ncols + jnp.arange(ncols)[None, :]
    row_coef = jnp.where(global_row < total_rows - 1, diffusivity[0, 0], jnp.float32(0.0))
    col_coef = jnp.where(global_col < total_cols - 1, diffusivity[1, 0], jnp.float32(0.0))
    coef_ext = margin(jnp.stack([row_coef, col_coef], 0), HALO)
    perturb = ensemble[:, :, 0].astype(jnp.float32)
    values = weight * perturb * vec
    near = coef_ext[:, HALO - 1 : HALO + nrows + 1, HALO - 1 : HALO + ncols + 1]
    for _ in range(2 * SWEEPS):
        values = diffuse(margin(values, 1), near[0], near[1])
    partial_sum = jnp.sum(perturb * weight * values, axis=0)
    summed = lax.psum(partial_sum, "mem")
    members = lax.axis_size("mem") * ensemble.shape[0]
    ens_part = summed / jnp.float32(members - 1)
    result = ens_weight * ens_part + static_weight * static_var[:, 0] * vec
    return result[:, None]


def solution(mesh):
    placed = (
        P(None, "tile", None, None),
        P("mem", None, "tile", None, None),
        P(None, "tile", None, None),
        P("tile", None, None),
        P(None, "tile", None, None),
    )
    return jax.shard_map(
        local, mesh=mesh, in_specs=placed, out_specs=P(None, "tile", None, None), check_vma=False
    )
```

profile of v0, /device:TPU:16, one launch (start us, length us, event | category | flops | bytes accessed | tf_op | source)
XLA Modules:
  0.0 661.0 jit_solution(13833720016262433344)
XLA Ops:
  7.6 9.0 %collective-permute-start.4 = (f32[2,2,1,256]{3,2,1,0:T(1,128)S(1)}, f32[2,2,1,256]{3,2,1,0:T(1,128)S(1)}, u32[]{:S(2)}, u32[]{:S(2)}) collective-permute-start(f32[2,2,1,256]{3,2,1,0:T(1,128)S(1)} %get-tuple-element.68), channel_id=1, source_target_pairs={{8,0},{9,1},{10,2},{11,3},{12,4},{13,5},{14,6},{15,7},{16,8},{17,9... | collective-permute-start | bytes 12296 | tf_op jit(solution)/shard_map/ppermute | solution.py:18
  16.6 2.0 collective-permute-start.5
  18.8 8.1 %collective-permute-done.5 = f32[2,2,1,256]{3,2,1,0:T(1,128)S(1)} collective-permute-done((f32[2,2,1,256]{3,2,1,0:T(1,128)S(1)}, f32[2,2,1,256]{3,2,1,0:T(1,128)S(1)}, u32[]{:S(2)}, u32[]{:S(2)}) %collective-permute-start.5) | collective-permute-done | bytes 4128 | tf_op jit(solution)/shard_map/ppermute | solution.py:18
  29.0 1.9 collective-permute-start.1
  30.9 7.8 %collective-permute-start = (f32[2,3,256]{2,1,0:T(4,128)S(1)}, f32[2,3,256]{2,1,0:T(4,128)S(1)}, u32[]{:S(2)}, u32[]{:S(2)}) collective-permute-start(f32[2,3,256]{2,1,0:T(4,128)S(1)} %get-tuple-element.73), channel_id=1, source_target_pairs={{0,8},{1,9},{2,10},{3,11},{4,12},{5,13},{6,14},{7,15},{8,16},{9,17... | collective-permute-start | bytes 18440 | tf_op jit(solution)/shard_map/ppermute | solution.py:18
  38.7 11.5 %collective-permute-start.6 = (f32[2,2,66,1]{3,2,1,0:T(8,128)S(1)}, f32[2,2,66,1]{3,2,1,0:T(8,128)S(1)}, u32[]{:S(2)}, u32[]{:S(2)}) collective-permute-start(f32[2,2,66,1]{3,2,1,0:T(8,128)S(1)} %get-tuple-element.35), channel_id=1, source_target_pairs={{1,0},{2,1},{3,2},{4,3},{5,4},{6,5},{7,6},{8,7},{9,8},{10,9},{11,1... | collective-permute-start | bytes 3176 | tf_op jit(solution)/shard_map/ppermute | solution.py:18
  52.9 1.9 collective-permute-start.2
  54.9 11.4 %collective-permute-done.2 = f32[2,70,3]{2,1,0:T(8,128)S(1)} collective-permute-done((f32[2,70,3]{2,1,0:T(8,128)S(1)}, f32[2,70,3]{2,1,0:T(8,128)S(1)}, u32[]{:S(2)}, u32[]{:S(2)}) %collective-permute-start.2) | collective-permute-done | bytes 1712 | tf_op jit(solution)/shard_map/ppermute | solution.py:18
  69.8 7.8 %collective-permute-start.9 = (f32[2,2,1,256]{3,2,1,0:T(1,128)S(1)}, f32[2,2,1,256]{3,2,1,0:T(1,128)S(1)}, u32[]{:S(2)}, u32[]{:S(2)}) collective-permute-start(f32[2,2,1,256]{3,2,1,0:T(1,128)S(1)} %get-tuple-element.65), channel_id=1, source_target_pairs={{0,8},{1,9},{2,10},{3,11},{4,12},{5,13},{6,14},{7,15},{8,16},{9,17... | collective-permute-start | bytes 12296 | tf_op jit(solution)/shard_map/ppermute | solution.py:18
  77.7 2.6 collective-permute-done.9
  82.3 11.1 %collective-permute-start.10 = (f32[2,2,66,1]{3,2,1,0:T(8,128)S(1)}, f32[2,2,66,1]{3,2,1,0:T(8,128)S(1)}, u32[]{:S(2)}, u32[]{:S(2)}) collective-permute-start(f32[2,2,66,1]{3,2,1,0:T(8,128)S(1)} %get-tuple-element.33), channel_id=1, source_target_pairs={{1,0},{2,1},{3,2},{4,3},{5,4},{6,5},{7,6},{8,7},{9,8},{10,9},{11,1... | collective-permute-start | bytes 3176 | tf_op jit(solution)/shard_map/ppermute | solution.py:18
  98.4 7.8 %collective-permute-start.13 = (f32[2,2,1,256]{3,2,1,0:T(1,128)S(1)}, f32[2,2,1,256]{3,2,1,0:T(1,128)S(1)}, u32[]{:S(2)}, u32[]{:S(2)}) collective-permute-start(f32[2,2,1,256]{3,2,1,0:T(1,128)S(1)} %get-tuple-element.63), channel_id=1, source_target_pairs={{0,8},{1,9},{2,10},{3,11},{4,12},{5,13},{6,14},{7,15},{8,16},{9,17... | collective-permute-start | bytes 12296 | tf_op jit(solution)/shard_map/ppermute | solution.py:18
  106.3 2.5 collective-permute-done.13
  110.8 11.1 %collective-permute-start.14 = (f32[2,2,66,1]{3,2,1,0:T(8,128)S(1)}, f32[2,2,66,1]{3,2,1,0:T(8,128)S(1)}, u32[]{:S(2)}, u32[]{:S(2)}) collective-permute-start(f32[2,2,66,1]{3,2,1,0:T(8,128)S(1)} %get-tuple-element.31), channel_id=1, source_target_pairs={{1,0},{2,1},{3,2},{4,3},{5,4},{6,5},{7,6},{8,7},{9,8},{10,9},{11,1... | collective-permute-start | bytes 3176 | tf_op jit(solution)/shard_map/ppermute | solution.py:18
  125.0 3.7 collective-permute-start.16
  128.8 6.0 collective-permute-start.17
  134.8 4.3 collective-permute-done.17
  141.1 11.1 %collective-permute-start.18 = (f32[2,2,66,1]{3,2,1,0:T(8,128)S(1)}, f32[2,2,66,1]{3,2,1,0:T(8,128)S(1)}, u32[]{:S(2)}, u32[]{:S(2)}) collective-permute-start(f32[2,2,66,1]{3,2,1,0:T(8,128)S(1)} %get-tuple-element.29), channel_id=1, source_target_pairs={{1,0},{2,1},{3,2},{4,3},{5,4},{6,5},{7,6},{8,7},{9,8},{10,9},{11,1... | collective-permute-start | bytes 3176 | tf_op jit(solution)/shard_map/ppermute | solution.py:18
  152.3 2.1 collective-permute-done.19
  155.4 2.3 collective-permute-start.20
  157.6 7.5 %collective-permute-start.21 = (f32[2,2,1,256]{3,2,1,0:T(1,128)S(1)}, f32[2,2,1,256]{3,2,1,0:T(1,128)S(1)}, u32[]{:S(2)}, u32[]{:S(2)}) collective-permute-start(f32[2,2,1,256]{3,2,1,0:T(1,128)S(1)} %get-tuple-element.59), channel_id=1, source_target_pairs={{0,8},{1,9},{2,10},{3,11},{4,12},{5,13},{6,14},{7,15},{8,16},{9,17... | collective-permute-start | bytes 12296 | tf_op jit(solution)/shard_map/ppermute | solution.py:18
  165.1 2.8 collective-permute-done.21
  170.0 11.1 %collective-permute-start.22 = (f32[2,2,66,1]{3,2,1,0:T(8,128)S(1)}, f32[2,2,66,1]{3,2,1,0:T(8,128)S(1)}, u32[]{:S(2)}, u32[]{:S(2)}) collective-permute-start(f32[2,2,66,1]{3,2,1,0:T(8,128)S(1)} %get-tuple-element.27), channel_id=1, source_target_pairs={{1,0},{2,1},{3,2},{4,3},{5,4},{6,5},{7,6},{8,7},{9,8},{10,9},{11,1... | collective-permute-start | bytes 3176 | tf_op jit(solution)/shard_map/ppermute | solution.py:18
  186.1 7.8 %collective-permute-start.25 = (f32[2,2,1,256]{3,2,1,0:T(1,128)S(1)}, f32[2,2,1,256]{3,2,1,0:T(1,128)S(1)}, u32[]{:S(2)}, u32[]{:S(2)}) collective-permute-start(f32[2,2,1,256]{3,2,1,0:T(1,128)S(1)} %get-tuple-element.57), channel_id=1, source_target_pairs={{0,8},{1,9},{2,10},{3,11},{4,12},{5,13},{6,14},{7,15},{8,16},{9,17... | collective-permute-start | bytes 12296 | tf_op jit(solution)/shard_map/ppermute | solution.py:18
  194.0 2.5 collective-permute-done.25
  198.5 11.1 %collective-permute-start.26 = (f32[2,2,66,1]{3,2,1,0:T(8,128)S(1)}, f32[2,2,66,1]{3,2,1,0:T(8,128)S(1)}, u32[]{:S(2)}, u32[]{:S(2)}) collective-permute-start(f32[2,2,66,1]{3,2,1,0:T(8,128)S(1)} %get-tuple-element.25), channel_id=1, source_target_pairs={{1,0},{2,1},{3,2},{4,3},{5,4},{6,5},{7,6},{8,7},{9,8},{10,9},{11,1... | collective-permute-start | bytes 3176 | tf_op jit(solution)/shard_map/ppermute | solution.py:18
  214.7 7.8 %collective-permute-start.29 = (f32[2,2,1,256]{3,2,1,0:T(1,128)S(1)}, f32[2,2,1,256]{3,2,1,0:T(1,128)S(1)}, u32[]{:S(2)}, u32[]{:S(2)}) collective-permute-start(f32[2,2,1,256]{3,2,1,0:T(1,128)S(1)} %get-tuple-element.55), channel_id=1, source_target_pairs={{0,8},{1,9},{2,10},{3,11},{4,12},{5,13},{6,14},{7,15},{8,16},{9,17... | collective-permute-start | bytes 12296 | tf_op jit(solution)/shard_map/ppermute | solution.py:18
  222.5 2.5 collective-permute-done.29
  227.0 11.1 %collective-permute-start.30 = (f32[2,2,66,1]{3,2,1,0:T(8,128)S(1)}, f32[2,2,66,1]{3,2,1,0:T(8,128)S(1)}, u32[]{:S(2)}, u32[]{:S(2)}) collective-permute-start(f32[2,2,66,1]{3,2,1,0:T(8,128)S(1)} %get-tuple-element.23), channel_id=1, source_target_pairs={{1,0},{2,1},{3,2},{4,3},{5,4},{6,5},{7,6},{8,7},{9,8},{10,9},{11,1... | collective-permute-start | bytes 3176 | tf_op jit(solution)/shard_map/ppermute | solution.py:18
  243.2 7.8 %collective-permute-start.33 = (f32[2,2,1,256]{3,2,1,0:T(1,128)S(1)}, f32[2,2,1,256]{3,2,1,0:T(1,128)S(1)}, u32[]{:S(2)}, u32[]{:S(2)}) collective-permute-start(f32[2,2,1,256]{3,2,1,0:T(1,128)S(1)} %get-tuple-element.53), channel_id=1, source_target_pairs={{0,8},{1,9},{2,10},{3,11},{4,12},{5,13},{6,14},{7,15},{8,16},{9,17... | collective-permute-start | bytes 12296 | tf_op jit(solution)/shard_map/ppermute | solution.py:18
  251.0 2.5 collective-permute-done.33
  255.6 11.1 %collective-permute-start.34 = (f32[2,2,66,1]{3,2,1,0:T(8,128)S(1)}, f32[2,2,66,1]{3,2,1,0:T(8,128)S(1)}, u32[]{:S(2)}, u32[]{:S(2)}) collective-permute-start(f32[2,2,66,1]{3,2,1,0:T(8,128)S(1)} %get-tuple-element.21), channel_id=1, source_target_pairs={{1,0},{2,1},{3,2},{4,3},{5,4},{6,5},{7,6},{8,7},{9,8},{10,9},{11,1... | collective-permute-start | bytes 3176 | tf_op jit(solution)/shard_map/ppermute | solution.py:18
  271.7 7.8 %collective-permute-start.37 = (f32[2,2,1,256]{3,2,1,0:T(1,128)S(1)}, f32[2,2,1,256]{3,2,1,0:T(1,128)S(1)}, u32[]{:S(2)}, u32[]{:S(2)}) collective-permute-start(f32[2,2,1,256]{3,2,1,0:T(1,128)S(1)} %get-tuple-element.51), channel_id=1, source_target_pairs={{0,8},{1,9},{2,10},{3,11},{4,12},{5,13},{6,14},{7,15},{8,16},{9,17... | collective-permute-start | bytes 12296 | tf_op jit(solution)/shard_map/ppermute | solution.py:18
  279.5 2.5 collective-permute-done.37
  284.1 11.1 %collective-permute-start.38 = (f32[2,2,66,1]{3,2,1,0:T(8,128)S(1)}, f32[2,2,66,1]{3,2,1,0:T(8,128)S(1)}, u32[]{:S(2)}, u32[]{:S(2)}) collective-permute-start(f32[2,2,66,1]{3,2,1,0:T(8,128)S(1)} %get-tuple-element.19), channel_id=1, source_target_pairs={{1,0},{2,1},{3,2},{4,3},{5,4},{6,5},{7,6},{8,7},{9,8},{10,9},{11,1... | collective-permute-start | bytes 3176 | tf_op jit(solution)/shard_map/ppermute | solution.py:18
  298.3 2.0 collective-permute-start.40
  300.3 7.8 %collective-permute-start.41 = (f32[2,2,1,256]{3,2,1,0:T(1,128)S(1)}, f32[2,2,1,256]{3,2,1,0:T(1,128)S(1)}, u32[]{:S(2)}, u32[]{:S(2)}) collective-permute-start(f32[2,2,1,256]{3,2,1,0:T(1,128)S(1)} %get-tuple-element.49), channel_id=1, source_target_pairs={{0,8},{1,9},{2,10},{3,11},{4,12},{5,13},{6,14},{7,15},{8,16},{9,17... | collective-permute-start | bytes 12296 | tf_op jit(solution)/shard_map/ppermute | solution.py:18
  308.1 2.5 collective-permute-done.41
  312.6 11.1 %collective-permute-start.42 = (f32[2,2,66,1]{3,2,1,0:T(8,128)S(1)}, f32[2,2,66,1]{3,2,1,0:T(8,128)S(1)}, u32[]{:S(2)}, u32[]{:S(2)}) collective-permute-start(f32[2,2,66,1]{3,2,1,0:T(8,128)S(1)} %get-tuple-element.17), channel_id=1, source_target_pairs={{1,0},{2,1},{3,2},{4,3},{5,4},{6,5},{7,6},{8,7},{9,8},{10,9},{11,1... | collective-permute-start | bytes 3176 | tf_op jit(solution)/shard_map/ppermute | solution.py:18
  326.9 2.0 collective-permute-start.44
  328.9 7.7 %collective-permute-start.45 = (f32[2,2,1,256]{3,2,1,0:T(1,128)S(1)}, f32[2,2,1,256]{3,2,1,0:T(1,128)S(1)}, u32[]{:S(2)}, u32[]{:S(2)}) collective-permute-start(f32[2,2,1,256]{3,2,1,0:T(1,128)S(1)} %get-tuple-element.47), channel_id=1, source_target_pairs={{0,8},{1,9},{2,10},{3,11},{4,12},{5,13},{6,14},{7,15},{8,16},{9,17... | collective-permute-start | bytes 12296 | tf_op jit(solution)/shard_map/ppermute | solution.py:18
  336.6 2.6 collective-permute-done.45
  341.3 11.1 %collective-permute-start.46 = (f32[2,2,66,1]{3,2,1,0:T(8,128)S(1)}, f32[2,2,66,1]{3,2,1,0:T(8,128)S(1)}, u32[]{:S(2)}, u32[]{:S(2)}) collective-permute-start(f32[2,2,66,1]{3,2,1,0:T(8,128)S(1)} %get-tuple-element.15), channel_id=1, source_target_pairs={{1,0},{2,1},{3,2},{4,3},{5,4},{6,5},{7,6},{8,7},{9,8},{10,9},{11,1... | collective-permute-start | bytes 3176 | tf_op jit(solution)/shard_map/ppermute | solution.py:18
  355.5 2.0 collective-permute-start.48
  357.5 7.7 %collective-permute-start.49 = (f32[2,2,1,256]{3,2,1,0:T(1,128)S(1)}, f32[2,2,1,256]{3,2,1,0:T(1,128)S(1)}, u32[]{:S(2)}, u32[]{:S(2)}) collective-permute-start(f32[2,2,1,256]{3,2,1,0:T(1,128)S(1)} %get-tuple-element.45), channel_id=1, source_target_pairs={{0,8},{1,9},{2,10},{3,11},{4,12},{5,13},{6,14},{7,15},{8,16},{9,17... | collective-permute-start | bytes 12296 | tf_op jit(solution)/shard_map/ppermute | solution.py:18
  365.3 2.6 collective-permute-done.49
  369.9 11.1 %collective-permute-start.50 = (f32[2,2,66,1]{3,2,1,0:T(8,128)S(1)}, f32[2,2,66,1]{3,2,1,0:T(8,128)S(1)}, u32[]{:S(2)}, u32[]{:S(2)}) collective-permute-start(f32[2,2,66,1]{3,2,1,0:T(8,128)S(1)} %get-tuple-element.13), channel_id=1, source_target_pairs={{1,0},{2,1},{3,2},{4,3},{5,4},{6,5},{7,6},{8,7},{9,8},{10,9},{11,1... | collective-permute-start | bytes 3176 | tf_op jit(solution)/shard_map/ppermute | solution.py:18
  384.1 2.0 collective-permute-start.52
  386.1 7.7 %collective-permute-start.53 = (f32[2,2,1,256]{3,2,1,0:T(1,128)S(1)}, f32[2,2,1,256]{3,2,1,0:T(1,128)S(1)}, u32[]{:S(2)}, u32[]{:S(2)}) collective-permute-start(f32[2,2,1,256]{3,2,1,0:T(1,128)S(1)} %get-tuple-element.43), channel_id=1, source_target_pairs={{0,8},{1,9},{2,10},{3,11},{4,12},{5,13},{6,14},{7,15},{8,16},{9,17... | collective-permute-start | bytes 12296 | tf_op jit(solution)/shard_map/ppermute | solution.py:18
  393.9 2.6 collective-permute-done.53
  398.5 11.1 %collective-permute-start.54 = (f32[2,2,66,1]{3,2,1,0:T(8,128)S(1)}, f32[2,2,66,1]{3,2,1,0:T(8,128)S(1)}, u32[]{:S(2)}, u32[]{:S(2)}) collective-permute-start(f32[2,2,66,1]{3,2,1,0:T(8,128)S(1)} %get-tuple-element.11), channel_id=1, source_target_pairs={{1,0},{2,1},{3,2},{4,3},{5,4},{6,5},{7,6},{8,7},{9,8},{10,9},{11,1... | collective-permute-start | bytes 3176 | tf_op jit(solution)/shard_map/ppermute | solution.py:18
  412.7 2.0 collective-permute-start.56
  414.8 7.7 %collective-permute-start.57 = (f32[2,2,1,256]{3,2,1,0:T(1,128)S(1)}, f32[2,2,1,256]{3,2,1,0:T(1,128)S(1)}, u32[]{:S(2)}, u32[]{:S(2)}) collective-permute-start(f32[2,2,1,256]{3,2,1,0:T(1,128)S(1)} %get-tuple-element.41), channel_id=1, source_target_pairs={{0,8},{1,9},{2,10},{3,11},{4,12},{5,13},{6,14},{7,15},{8,16},{9,17... | collective-permute-start | bytes 12296 | tf_op jit(solution)/shard_map/ppermute | solution.py:18
  422.5 2.6 collective-permute-done.57
  427.1 11.1 %collective-permute-start.58 = (f32[2,2,66,1]{3,2,1,0:T(8,128)S(1)}, f32[2,2,66,1]{3,2,1,0:T(8,128)S(1)}, u32[]{:S(2)}, u32[]{:S(2)}) collective-permute-start(f32[2,2,66,1]{3,2,1,0:T(8,128)S(1)} %get-tuple-element.9), channel_id=1, source_target_pairs={{1,0},{2,1},{3,2},{4,3},{5,4},{6,5},{7,6},{8,7},{9,8},{10,9},{11,1... | collective-permute-start | bytes 3176 | tf_op jit(solution)/shard_map/ppermute | solution.py:18
  441.4 2.0 collective-permute-start.60
  443.4 7.7 %collective-permute-start.61 = (f32[2,2,1,256]{3,2,1,0:T(1,128)S(1)}, f32[2,2,1,256]{3,2,1,0:T(1,128)S(1)}, u32[]{:S(2)}, u32[]{:S(2)}) collective-permute-start(f32[2,2,1,256]{3,2,1,0:T(1,128)S(1)} %get-tuple-element.39), channel_id=1, source_target_pairs={{0,8},{1,9},{2,10},{3,11},{4,12},{5,13},{6,14},{7,15},{8,16},{9,17... | collective-permute-start | bytes 12296 | tf_op jit(solution)/shard_map/ppermute | solution.py:18
  451.1 2.6 collective-permute-done.61
  455.8 11.1 %collective-permute-start.62 = (f32[2,2,66,1]{3,2,1,0:T(8,128)S(1)}, f32[2,2,66,1]{3,2,1,0:T(8,128)S(1)}, u32[]{:S(2)}, u32[]{:S(2)}) collective-permute-start(f32[2,2,66,1]{3,2,1,0:T(8,128)S(1)} %get-tuple-element.7), channel_id=1, source_target_pairs={{1,0},{2,1},{3,2},{4,3},{5,4},{6,5},{7,6},{8,7},{9,8},{10,9},{11,1... | collective-permute-start | bytes 3176 | tf_op jit(solution)/shard_map/ppermute | solution.py:18
  470.0 2.0 collective-permute-start.64
  472.0 7.7 %collective-permute-start.65 = (f32[2,2,1,256]{3,2,1,0:T(1,128)S(1)}, f32[2,2,1,256]{3,2,1,0:T(1,128)S(1)}, u32[]{:S(2)}, u32[]{:S(2)}) collective-permute-start(f32[2,2,1,256]{3,2,1,0:T(1,128)S(1)} %get-tuple-element.37), channel_id=1, source_target_pairs={{0,8},{1,9},{2,10},{3,11},{4,12},{5,13},{6,14},{7,15},{8,16},{9,17... | collective-permute-start | bytes 12296 | tf_op jit(solution)/shard_map/ppermute | solution.py:18
  479.8 2.6 collective-permute-done.65
  484.4 11.1 %collective-permute-start.66 = (f32[2,2,66,1]{3,2,1,0:T(8,128)S(1)}, f32[2,2,66,1]{3,2,1,0:T(8,128)S(1)}, u32[]{:S(2)}, u32[]{:S(2)}) collective-permute-start(f32[2,2,66,1]{3,2,1,0:T(8,128)S(1)} %get-tuple-element.5), channel_id=1, source_target_pairs={{1,0},{2,1},{3,2},{4,3},{5,4},{6,5},{7,6},{8,7},{9,8},{10,9},{11,1... | collective-permute-start | bytes 3176 | tf_op jit(solution)/shard_map/ppermute | solution.py:18
  499.3 153.3 %all-reduce.2.cloned.1.call-done = f32[2,64,256]{2,1,0:T(8,128)} async-done(((f32[2,64,256]{2,1,0:T(8,128)}), f32[2,64,256]{2,1,0:T(8,128)}) %all-reduce.2.cloned.1.call-update) | async-done | bytes 131088 | tf_op jit(solution)/shard_map/psum | solution.py:66
  (227 shorter events, 95.3 us)
Async XLA Ops:
  6.5 646.0 %all-reduce.2.cloned.1.call-start = ((), (), s32[]{:S(2)}) async-start(), calls=%async_computation | async-start | bytes 262144 | tf_op jit(solution)/shard_map/psum | solution.py:66
  7.6 11.2 %collective-permute-start.4 = (f32[2,2,1,256]{3,2,1,0:T(1,128)S(1)}, f32[2,2,1,256]{3,2,1,0:T(1,128)S(1)}, u32[]{:S(2)}, u32[]{:S(2)}) collective-permute-start(f32[2,2,1,256]{3,2,1,0:T(1,128)S(1)} %get-tuple-element.68), channel_id=1, source_target_pairs={{8,0},{9,1},{10,2},{11,3},{12,4},{13,5},{14,6},{15,7},{16,8},{17,9... | collective-permute-start | bytes 12296 | tf_op jit(solution)/shard_map/ppermute | solution.py:18
  16.6 10.3 %collective-permute-start.5 = (f32[2,2,1,256]{3,2,1,0:T(1,128)S(1)}, f32[2,2,1,256]{3,2,1,0:T(1,128)S(1)}, u32[]{:S(2)}, u32[]{:S(2)}) collective-permute-start(f32[2,2,1,256]{3,2,1,0:T(1,128)S(1)} %get-tuple-element.67), channel_id=1, source_target_pairs={{0,8},{1,9},{2,10},{3,11},{4,12},{5,13},{6,14},{7,15},{8,16},{9,17... | collective-permute-start | bytes 12296 | tf_op jit(solution)/shard_map/ppermute | solution.py:18
  27.0 23.2 %collective-permute-start.7 = (f32[2,2,66,1]{3,2,1,0:T(8,128)S(1)}, f32[2,2,66,1]{3,2,1,0:T(8,128)S(1)}, u32[]{:S(2)}, u32[]{:S(2)}) collective-permute-start(f32[2,2,66,1]{3,2,1,0:T(8,128)S(1)} %get-tuple-element.36), channel_id=1, source_target_pairs={{0,1},{1,2},{2,3},{3,4},{4,5},{5,6},{6,7},{7,8},{8,9},{9,10},{10,1... | collective-permute-start | bytes 3176 | tf_op jit(solution)/shard_map/ppermute | solution.py:18
  29.0 21.3 %collective-permute-start.1 = (f32[2,3,256]{2,1,0:T(4,128)S(1)}, f32[2,3,256]{2,1,0:T(4,128)S(1)}, u32[]{:S(2)}, u32[]{:S(2)}) collective-permute-start(f32[2,3,256]{2,1,0:T(4,128)S(1)} %get-tuple-element.74), channel_id=1, source_target_pairs={{8,0},{9,1},{10,2},{11,3},{12,4},{13,5},{14,6},{15,7},{16,8},{17,9... | collective-permute-start | bytes 18440 | tf_op jit(solution)/shard_map/ppermute | solution.py:18
  30.9 19.4 %collective-permute-start = (f32[2,3,256]{2,1,0:T(4,128)S(1)}, f32[2,3,256]{2,1,0:T(4,128)S(1)}, u32[]{:S(2)}, u32[]{:S(2)}) collective-permute-start(f32[2,3,256]{2,1,0:T(4,128)S(1)} %get-tuple-element.73), channel_id=1, source_target_pairs={{0,8},{1,9},{2,10},{3,11},{4,12},{5,13},{6,14},{7,15},{8,16},{9,17... | collective-permute-start | bytes 18440 | tf_op jit(solution)/shard_map/ppermute | solution.py:18
  38.7 14.1 %collective-permute-start.6 = (f32[2,2,66,1]{3,2,1,0:T(8,128)S(1)}, f32[2,2,66,1]{3,2,1,0:T(8,128)S(1)}, u32[]{:S(2)}, u32[]{:S(2)}) collective-permute-start(f32[2,2,66,1]{3,2,1,0:T(8,128)S(1)} %get-tuple-element.35), channel_id=1, source_target_pairs={{1,0},{2,1},{3,2},{4,3},{5,4},{6,5},{7,6},{8,7},{9,8},{10,9},{11,1... | collective-permute-start | bytes 3176 | tf_op jit(solution)/shard_map/ppermute | solution.py:18
  52.9 13.4 %collective-permute-start.2 = (f32[2,70,3]{2,1,0:T(8,128)S(1)}, f32[2,70,3]{2,1,0:T(8,128)S(1)}, u32[]{:S(2)}, u32[]{:S(2)}) collective-permute-start(f32[2,70,3]{2,1,0:T(8,128)S(1)} %get-tuple-element.71), channel_id=1, source_target_pairs={{0,1},{1,2},{2,3},{3,4},{4,5},{5,6},{6,7},{7,8},{8,9},{9,10},{10,1... | collective-permute-start | bytes 5048 | tf_op jit(solution)/shard_map/ppermute | solution.py:18
  67.9 9.8 %collective-permute-start.8 = (f32[2,2,1,256]{3,2,1,0:T(1,128)S(1)}, f32[2,2,1,256]{3,2,1,0:T(1,128)S(1)}, u32[]{:S(2)}, u32[]{:S(2)}) collective-permute-start(f32[2,2,1,256]{3,2,1,0:T(1,128)S(1)} %get-tuple-element.66), channel_id=1, source_target_pairs={{8,0},{9,1},{10,2},{11,3},{12,4},{13,5},{14,6},{15,7},{16,8},{17,9... | collective-permute-start | bytes 12296 | tf_op jit(solution)/shard_map/ppermute | solution.py:18
  69.8 10.4 %collective-permute-start.9 = (f32[2,2,1,256]{3,2,1,0:T(1,128)S(1)}, f32[2,2,1,256]{3,2,1,0:T(1,128)S(1)}, u32[]{:S(2)}, u32[]{:S(2)}) collective-permute-start(f32[2,2,1,256]{3,2,1,0:T(1,128)S(1)} %get-tuple-element.65), channel_id=1, source_target_pairs={{0,8},{1,9},{2,10},{3,11},{4,12},{5,13},{6,14},{7,15},{8,16},{9,17... | collective-permute-start | bytes 12296 | tf_op jit(solution)/shard_map/ppermute | solution.py:18
  80.4 14.1 %collective-permute-start.11 = (f32[2,2,66,1]{3,2,1,0:T(8,128)S(1)}, f32[2,2,66,1]{3,2,1,0:T(8,128)S(1)}, u32[]{:S(2)}, u32[]{:S(2)}) collective-permute-start(f32[2,2,66,1]{3,2,1,0:T(8,128)S(1)} %get-tuple-element.34), channel_id=1, source_target_pairs={{0,1},{1,2},{2,3},{3,4},{4,5},{5,6},{6,7},{7,8},{8,9},{9,10},{10,1... | collective-permute-start | bytes 3176 | tf_op jit(solution)/shard_map/ppermute | solution.py:18
  82.3 13.8 %collective-permute-start.10 = (f32[2,2,66,1]{3,2,1,0:T(8,128)S(1)}, f32[2,2,66,1]{3,2,1,0:T(8,128)S(1)}, u32[]{:S(2)}, u32[]{:S(2)}) collective-permute-start(f32[2,2,66,1]{3,2,1,0:T(8,128)S(1)} %get-tuple-element.33), channel_id=1, source_target_pairs={{1,0},{2,1},{3,2},{4,3},{5,4},{6,5},{7,6},{8,7},{9,8},{10,9},{11,1... | collective-permute-start | bytes 3176 | tf_op jit(solution)/shard_map/ppermute | solution.py:18
  96.5 9.8 %collective-permute-start.12 = (f32[2,2,1,256]{3,2,1,0:T(1,128)S(1)}, f32[2,2,1,256]{3,2,1,0:T(1,128)S(1)}, u32[]{:S(2)}, u32[]{:S(2)}) collective-permute-start(f32[2,2,1,256]{3,2,1,0:T(1,128)S(1)} %get-tuple-element.64), channel_id=1, source_target_pairs={{8,0},{9,1},{10,2},{11,3},{12,4},{13,5},{14,6},{15,7},{16,8},{17,9... | collective-permute-start | bytes 12296 | tf_op jit(solution)/shard_map/ppermute | solution.py:18
  98.4 10.3 %collective-permute-start.13 = (f32[2,2,1,256]{3,2,1,0:T(1,128)S(1)}, f32[2,2,1,256]{3,2,1,0:T(1,128)S(1)}, u32[]{:S(2)}, u32[]{:S(2)}) collective-permute-start(f32[2,2,1,256]{3,2,1,0:T(1,128)S(1)} %get-tuple-element.63), channel_id=1, source_target_pairs={{0,8},{1,9},{2,10},{3,11},{4,12},{5,13},{6,14},{7,15},{8,16},{9,17... | collective-permute-start | bytes 12296 | tf_op jit(solution)/shard_map/ppermute | solution.py:18
  108.9 14.1 %collective-permute-start.15 = (f32[2,2,66,1]{3,2,1,0:T(8,128)S(1)}, f32[2,2,66,1]{3,2,1,0:T(8,128)S(1)}, u32[]{:S(2)}, u32[]{:S(2)}) collective-permute-start(f32[2,2,66,1]{3,2,1,0:T(8,128)S(1)} %get-tuple-element.32), channel_id=1, source_target_pairs={{0,1},{1,2},{2,3},{3,4},{4,5},{5,6},{6,7},{7,8},{8,9},{9,10},{10,1... | collective-permute-start | bytes 3176 | tf_op jit(solution)/shard_map/ppermute | solution.py:18
  110.8 13.8 %collective-permute-start.14 = (f32[2,2,66,1]{3,2,1,0:T(8,128)S(1)}, f32[2,2,66,1]{3,2,1,0:T(8,128)S(1)}, u32[]{:S(2)}, u32[]{:S(2)}) collective-permute-start(f32[2,2,66,1]{3,2,1,0:T(8,128)S(1)} %get-tuple-element.31), channel_id=1, source_target_pairs={{1,0},{2,1},{3,2},{4,3},{5,4},{6,5},{7,6},{8,7},{9,8},{10,9},{11,1... | collective-permute-start | bytes 3176 | tf_op jit(solution)/shard_map/ppermute | solution.py:18
  125.0 9.8 %collective-permute-start.16 = (f32[2,2,1,256]{3,2,1,0:T(1,128)S(1)}, f32[2,2,1,256]{3,2,1,0:T(1,128)S(1)}, u32[]{:S(2)}, u32[]{:S(2)}) collective-permute-start(f32[2,2,1,256]{3,2,1,0:T(1,128)S(1)} %get-tuple-element.62), channel_id=1, source_target_pairs={{8,0},{9,1},{10,2},{11,3},{12,4},{13,5},{14,6},{15,7},{16,8},{17,9... | collective-permute-start | bytes 12296 | tf_op jit(solution)/shard_map/ppermute | solution.py:18
  128.8 10.3 %collective-permute-start.17 = (f32[2,2,1,256]{3,2,1,0:T(1,128)S(1)}, f32[2,2,1,256]{3,2,1,0:T(1,128)S(1)}, u32[]{:S(2)}, u32[]{:S(2)}) collective-permute-start(f32[2,2,1,256]{3,2,1,0:T(1,128)S(1)} %get-tuple-element.61), channel_id=1, source_target_pairs={{0,8},{1,9},{2,10},{3,11},{4,12},{5,13},{6,14},{7,15},{8,16},{9,17... | collective-permute-start | bytes 12296 | tf_op jit(solution)/shard_map/ppermute | solution.py:18
  139.2 15.2 %collective-permute-start.19 = (f32[2,2,66,1]{3,2,1,0:T(8,128)S(1)}, f32[2,2,66,1]{3,2,1,0:T(8,128)S(1)}, u32[]{:S(2)}, u32[]{:S(2)}) collective-permute-start(f32[2,2,66,1]{3,2,1,0:T(8,128)S(1)} %get-tuple-element.30), channel_id=1, source_target_pairs={{0,1},{1,2},{2,3},{3,4},{4,5},{5,6},{6,7},{7,8},{8,9},{9,10},{10,1... | collective-permute-start | bytes 3176 | tf_op jit(solution)/shard_map/ppermute | solution.py:18
  141.1 13.8 %collective-permute-start.18 = (f32[2,2,66,1]{3,2,1,0:T(8,128)S(1)}, f32[2,2,66,1]{3,2,1,0:T(8,128)S(1)}, u32[]{:S(2)}, u32[]{:S(2)}) collective-permute-start(f32[2,2,66,1]{3,2,1,0:T(8,128)S(1)} %get-tuple-element.29), channel_id=1, source_target_pairs={{1,0},{2,1},{3,2},{4,3},{5,4},{6,5},{7,6},{8,7},{9,8},{10,9},{11,1... | collective-permute-start | bytes 3176 | tf_op jit(solution)/shard_map/ppermute | solution.py:18
  155.4 9.8 %collective-permute-start.20 = (f32[2,2,1,256]{3,2,1,0:T(1,128)S(1)}, f32[2,2,1,256]{3,2,1,0:T(1,128)S(1)}, u32[]{:S(2)}, u32[]{:S(2)}) collective-permute-start(f32[2,2,1,256]{3,2,1,0:T(1,128)S(1)} %get-tuple-element.60), channel_id=1, source_target_pairs={{8,0},{9,1},{10,2},{11,3},{12,4},{13,5},{14,6},{15,7},{16,8},{17,9... | collective-permute-start | bytes 12296 | tf_op jit(solution)/shard_map/ppermute | solution.py:18
  157.6 10.3 %collective-permute-start.21 = (f32[2,2,1,256]{3,2,1,0:T(1,128)S(1)}, f32[2,2,1,256]{3,2,1,0:T(1,128)S(1)}, u32[]{:S(2)}, u32[]{:S(2)}) collective-permute-start(f32[2,2,1,256]{3,2,1,0:T(1,128)S(1)} %get-tuple-element.59), channel_id=1, source_target_pairs={{0,8},{1,9},{2,10},{3,11},{4,12},{5,13},{6,14},{7,15},{8,16},{9,17... | collective-permute-start | bytes 12296 | tf_op jit(solution)/shard_map/ppermute | solution.py:18
  168.1 14.5 %collective-permute-start.23 = (f32[2,2,66,1]{3,2,1,0:T(8,128)S(1)}, f32[2,2,66,1]{3,2,1,0:T(8,128)S(1)}, u32[]{:S(2)}, u32[]{:S(2)}) collective-permute-start(f32[2,2,66,1]{3,2,1,0:T(8,128)S(1)} %get-tuple-element.28), channel_id=1, source_target_pairs={{0,1},{1,2},{2,3},{3,4},{4,5},{5,6},{6,7},{7,8},{8,9},{9,10},{10,1... | collective-permute-start | bytes 3176 | tf_op jit(solution)/shard_map/ppermute | solution.py:18
  170.0 13.8 %collective-permute-start.22 = (f32[2,2,66,1]{3,2,1,0:T(8,128)S(1)}, f32[2,2,66,1]{3,2,1,0:T(8,128)S(1)}, u32[]{:S(2)}, u32[]{:S(2)}) collective-permute-start(f32[2,2,66,1]{3,2,1,0:T(8,128)S(1)} %get-tuple-element.27), channel_id=1, source_target_pairs={{1,0},{2,1},{3,2},{4,3},{5,4},{6,5},{7,6},{8,7},{9,8},{10,9},{11,1... | collective-permute-start | bytes 3176 | tf_op jit(solution)/shard_map/ppermute | solution.py:18
  184.2 9.8 %collective-permute-start.24 = (f32[2,2,1,256]{3,2,1,0:T(1,128)S(1)}, f32[2,2,1,256]{3,2,1,0:T(1,128)S(1)}, u32[]{:S(2)}, u32[]{:S(2)}) collective-permute-start(f32[2,2,1,256]{3,2,1,0:T(1,128)S(1)} %get-tuple-element.58), channel_id=1, source_target_pairs={{8,0},{9,1},{10,2},{11,3},{12,4},{13,5},{14,6},{15,7},{16,8},{17,9... | collective-permute-start | bytes 12296 | tf_op jit(solution)/shard_map/ppermute | solution.py:18
  186.1 10.3 %collective-permute-start.25 = (f32[2,2,1,256]{3,2,1,0:T(1,128)S(1)}, f32[2,2,1,256]{3,2,1,0:T(1,128)S(1)}, u32[]{:S(2)}, u32[]{:S(2)}) collective-permute-start(f32[2,2,1,256]{3,2,1,0:T(1,128)S(1)} %get-tuple-element.57), channel_id=1, source_target_pairs={{0,8},{1,9},{2,10},{3,11},{4,12},{5,13},{6,14},{7,15},{8,16},{9,17... | collective-permute-start | bytes 12296 | tf_op jit(solution)/shard_map/ppermute | solution.py:18
  196.6 14.1 %collective-permute-start.27 = (f32[2,2,66,1]{3,2,1,0:T(8,128)S(1)}, f32[2,2,66,1]{3,2,1,0:T(8,128)S(1)}, u32[]{:S(2)}, u32[]{:S(2)}) collective-permute-start(f32[2,2,66,1]{3,2,1,0:T(8,128)S(1)} %get-tuple-element.26), channel_id=1, source_target_pairs={{0,1},{1,2},{2,3},{3,4},{4,5},{5,6},{6,7},{7,8},{8,9},{9,10},{10,1... | collective-permute-start | bytes 3176 | tf_op jit(solution)/shard_map/ppermute | solution.py:18
  198.5 13.8 %collective-permute-start.26 = (f32[2,2,66,1]{3,2,1,0:T(8,128)S(1)}, f32[2,2,66,1]{3,2,1,0:T(8,128)S(1)}, u32[]{:S(2)}, u32[]{:S(2)}) collective-permute-start(f32[2,2,66,1]{3,2,1,0:T(8,128)S(1)} %get-tuple-element.25), channel_id=1, source_target_pairs={{1,0},{2,1},{3,2},{4,3},{5,4},{6,5},{7,6},{8,7},{9,8},{10,9},{11,1... | collective-permute-start | bytes 3176 | tf_op jit(solution)/shard_map/ppermute | solution.py:18
  212.7 9.8 %collective-permute-start.28 = (f32[2,2,1,256]{3,2,1,0:T(1,128)S(1)}, f32[2,2,1,256]{3,2,1,0:T(1,128)S(1)}, u32[]{:S(2)}, u32[]{:S(2)}) collective-permute-start(f32[2,2,1,256]{3,2,1,0:T(1,128)S(1)} %get-tuple-element.56), channel_id=1, source_target_pairs={{8,0},{9,1},{10,2},{11,3},{12,4},{13,5},{14,6},{15,7},{16,8},{17,9... | collective-permute-start | bytes 12296 | tf_op jit(solution)/shard_map/ppermute | solution.py:18
  214.7 10.3 %collective-permute-start.29 = (f32[2,2,1,256]{3,2,1,0:T(1,128)S(1)}, f32[2,2,1,256]{3,2,1,0:T(1,128)S(1)}, u32[]{:S(2)}, u32[]{:S(2)}) collective-permute-start(f32[2,2,1,256]{3,2,1,0:T(1,128)S(1)} %get-tuple-element.55), channel_id=1, source_target_pairs={{0,8},{1,9},{2,10},{3,11},{4,12},{5,13},{6,14},{7,15},{8,16},{9,17... | collective-permute-start | bytes 12296 | tf_op jit(solution)/shard_map/ppermute | solution.py:18
  225.1 14.1 %collective-permute-start.31 = (f32[2,2,66,1]{3,2,1,0:T(8,128)S(1)}, f32[2,2,66,1]{3,2,1,0:T(8,128)S(1)}, u32[]{:S(2)}, u32[]{:S(2)}) collective-permute-start(f32[2,2,66,1]{3,2,1,0:T(8,128)S(1)} %get-tuple-element.24), channel_id=1, source_target_pairs={{0,1},{1,2},{2,3},{3,4},{4,5},{5,6},{6,7},{7,8},{8,9},{9,10},{10,1... | collective-permute-start | bytes 3176 | tf_op jit(solution)/shard_map/ppermute | solution.py:18
  227.0 13.8 %collective-permute-start.30 = (f32[2,2,66,1]{3,2,1,0:T(8,128)S(1)}, f32[2,2,66,1]{3,2,1,0:T(8,128)S(1)}, u32[]{:S(2)}, u32[]{:S(2)}) collective-permute-start(f32[2,2,66,1]{3,2,1,0:T(8,128)S(1)} %get-tuple-element.23), channel_id=1, source_target_pairs={{1,0},{2,1},{3,2},{4,3},{5,4},{6,5},{7,6},{8,7},{9,8},{10,9},{11,1... | collective-permute-start | bytes 3176 | tf_op jit(solution)/shard_map/ppermute | solution.py:18
  241.2 9.8 %collective-permute-start.32 = (f32[2,2,1,256]{3,2,1,0:T(1,128)S(1)}, f32[2,2,1,256]{3,2,1,0:T(1,128)S(1)}, u32[]{:S(2)}, u32[]{:S(2)}) collective-permute-start(f32[2,2,1,256]{3,2,1,0:T(1,128)S(1)} %get-tuple-element.54), channel_id=1, source_target_pairs={{8,0},{9,1},{10,2},{11,3},{12,4},{13,5},{14,6},{15,7},{16,8},{17,9... | collective-permute-start | bytes 12296 | tf_op jit(solution)/shard_map/ppermute | solution.py:18
  243.2 10.3 %collective-permute-start.33 = (f32[2,2,1,256]{3,2,1,0:T(1,128)S(1)}, f32[2,2,1,256]{3,2,1,0:T(1,128)S(1)}, u32[]{:S(2)}, u32[]{:S(2)}) collective-permute-start(f32[2,2,1,256]{3,2,1,0:T(1,128)S(1)} %get-tuple-element.53), channel_id=1, source_target_pairs={{0,8},{1,9},{2,10},{3,11},{4,12},{5,13},{6,14},{7,15},{8,16},{9,17... | collective-permute-start | bytes 12296 | tf_op jit(solution)/shard_map/ppermute | solution.py:18
  253.6 14.1 %collective-permute-start.35 = (f32[2,2,66,1]{3,2,1,0:T(8,128)S(1)}, f32[2,2,66,1]{3,2,1,0:T(8,128)S(1)}, u32[]{:S(2)}, u32[]{:S(2)}) collective-permute-start(f32[2,2,66,1]{3,2,1,0:T(8,128)S(1)} %get-tuple-element.22), channel_id=1, source_target_pairs={{0,1},{1,2},{2,3},{3,4},{4,5},{5,6},{6,7},{7,8},{8,9},{9,10},{10,1... | collective-permute-start | bytes 3176 | tf_op jit(solution)/shard_map/ppermute | solution.py:18
  255.6 13.8 %collective-permute-start.34 = (f32[2,2,66,1]{3,2,1,0:T(8,128)S(1)}, f32[2,2,66,1]{3,2,1,0:T(8,128)S(1)}, u32[]{:S(2)}, u32[]{:S(2)}) collective-permute-start(f32[2,2,66,1]{3,2,1,0:T(8,128)S(1)} %get-tuple-element.21), channel_id=1, source_target_pairs={{1,0},{2,1},{3,2},{4,3},{5,4},{6,5},{7,6},{8,7},{9,8},{10,9},{11,1... | collective-permute-start | bytes 3176 | tf_op jit(solution)/shard_map/ppermute | solution.py:18
  269.8 9.8 %collective-permute-start.36 = (f32[2,2,1,256]{3,2,1,0:T(1,128)S(1)}, f32[2,2,1,256]{3,2,1,0:T(1,128)S(1)}, u32[]{:S(2)}, u32[]{:S(2)}) collective-permute-start(f32[2,2,1,256]{3,2,1,0:T(1,128)S(1)} %get-tuple-element.52), channel_id=1, source_target_pairs={{8,0},{9,1},{10,2},{11,3},{12,4},{13,5},{14,6},{15,7},{16,8},{17,9... | collective-permute-start | bytes 12296 | tf_op jit(solution)/shard_map/ppermute | solution.py:18
  271.7 10.3 %collective-permute-start.37 = (f32[2,2,1,256]{3,2,1,0:T(1,128)S(1)}, f32[2,2,1,256]{3,2,1,0:T(1,128)S(1)}, u32[]{:S(2)}, u32[]{:S(2)}) collective-permute-start(f32[2,2,1,256]{3,2,1,0:T(1,128)S(1)} %get-tuple-element.51), channel_id=1, source_target_pairs={{0,8},{1,9},{2,10},{3,11},{4,12},{5,13},{6,14},{7,15},{8,16},{9,17... | collective-permute-start | bytes 12296 | tf_op jit(solution)/shard_map/ppermute | solution.py:18
  282.1 14.1 %collective-permute-start.39 = (f32[2,2,66,1]{3,2,1,0:T(8,128)S(1)}, f32[2,2,66,1]{3,2,1,0:T(8,128)S(1)}, u32[]{:S(2)}, u32[]{:S(2)}) collective-permute-start(f32[2,2,66,1]{3,2,1,0:T(8,128)S(1)} %get-tuple-element.20), channel_id=1, source_target_pairs={{0,1},{1,2},{2,3},{3,4},{4,5},{5,6},{6,7},{7,8},{8,9},{9,10},{10,1... | collective-permute-start | bytes 3176 | tf_op jit(solution)/shard_map/ppermute | solution.py:18
  284.1 13.8 %collective-permute-start.38 = (f32[2,2,66,1]{3,2,1,0:T(8,128)S(1)}, f32[2,2,66,1]{3,2,1,0:T(8,128)S(1)}, u32[]{:S(2)}, u32[]{:S(2)}) collective-permute-start(f32[2,2,66,1]{3,2,1,0:T(8,128)S(1)} %get-tuple-element.19), channel_id=1, source_target_pairs={{1,0},{2,1},{3,2},{4,3},{5,4},{6,5},{7,6},{8,7},{9,8},{10,9},{11,1... | collective-permute-start | bytes 3176 | tf_op jit(solution)/shard_map/ppermute | solution.py:18
  298.3 9.8 %collective-permute-start.40 = (f32[2,2,1,256]{3,2,1,0:T(1,128)S(1)}, f32[2,2,1,256]{3,2,1,0:T(1,128)S(1)}, u32[]{:S(2)}, u32[]{:S(2)}) collective-permute-start(f32[2,2,1,256]{3,2,1,0:T(1,128)S(1)} %get-tuple-element.50), channel_id=1, source_target_pairs={{8,0},{9,1},{10,2},{11,3},{12,4},{13,5},{14,6},{15,7},{16,8},{17,9... | collective-permute-start | bytes 12296 | tf_op jit(solution)/shard_map/ppermute | solution.py:18
  300.3 10.3 %collective-permute-start.41 = (f32[2,2,1,256]{3,2,1,0:T(1,128)S(1)}, f32[2,2,1,256]{3,2,1,0:T(1,128)S(1)}, u32[]{:S(2)}, u32[]{:S(2)}) collective-permute-start(f32[2,2,1,256]{3,2,1,0:T(1,128)S(1)} %get-tuple-element.49), channel_id=1, source_target_pairs={{0,8},{1,9},{2,10},{3,11},{4,12},{5,13},{6,14},{7,15},{8,16},{9,17... | collective-permute-start | bytes 12296 | tf_op jit(solution)/shard_map/ppermute | solution.py:18
  310.7 14.2 %collective-permute-start.43 = (f32[2,2,66,1]{3,2,1,0:T(8,128)S(1)}, f32[2,2,66,1]{3,2,1,0:T(8,128)S(1)}, u32[]{:S(2)}, u32[]{:S(2)}) collective-permute-start(f32[2,2,66,1]{3,2,1,0:T(8,128)S(1)} %get-tuple-element.18), channel_id=1, source_target_pairs={{0,1},{1,2},{2,3},{3,4},{4,5},{5,6},{6,7},{7,8},{8,9},{9,10},{10,1... | collective-permute-start | bytes 3176 | tf_op jit(solution)/shard_map/ppermute | solution.py:18
  312.6 13.8 %collective-permute-start.42 = (f32[2,2,66,1]{3,2,1,0:T(8,128)S(1)}, f32[2,2,66,1]{3,2,1,0:T(8,128)S(1)}, u32[]{:S(2)}, u32[]{:S(2)}) collective-permute-start(f32[2,2,66,1]{3,2,1,0:T(8,128)S(1)} %get-tuple-element.17), channel_id=1, source_target_pairs={{1,0},{2,1},{3,2},{4,3},{5,4},{6,5},{7,6},{8,7},{9,8},{10,9},{11,1... | collective-permute-start | bytes 3176 | tf_op jit(solution)/shard_map/ppermute | solution.py:18
  326.9 9.8 %collective-permute-start.44 = (f32[2,2,1,256]{3,2,1,0:T(1,128)S(1)}, f32[2,2,1,256]{3,2,1,0:T(1,128)S(1)}, u32[]{:S(2)}, u32[]{:S(2)}) collective-permute-start(f32[2,2,1,256]{3,2,1,0:T(1,128)S(1)} %get-tuple-element.48), channel_id=1, source_target_pairs={{8,0},{9,1},{10,2},{11,3},{12,4},{13,5},{14,6},{15,7},{16,8},{17,9... | collective-permute-start | bytes 12296 | tf_op jit(solution)/shard_map/ppermute | solution.py:18
  328.9 10.3 %collective-permute-start.45 = (f32[2,2,1,256]{3,2,1,0:T(1,128)S(1)}, f32[2,2,1,256]{3,2,1,0:T(1,128)S(1)}, u32[]{:S(2)}, u32[]{:S(2)}) collective-permute-start(f32[2,2,1,256]{3,2,1,0:T(1,128)S(1)} %get-tuple-element.47), channel_id=1, source_target_pairs={{0,8},{1,9},{2,10},{3,11},{4,12},{5,13},{6,14},{7,15},{8,16},{9,17... | collective-permute-start | bytes 12296 | tf_op jit(solution)/shard_map/ppermute | solution.py:18
  339.3 14.2 %collective-permute-start.47 = (f32[2,2,66,1]{3,2,1,0:T(8,128)S(1)}, f32[2,2,66,1]{3,2,1,0:T(8,128)S(1)}, u32[]{:S(2)}, u32[]{:S(2)}) collective-permute-start(f32[2,2,66,1]{3,2,1,0:T(8,128)S(1)} %get-tuple-element.16), channel_id=1, source_target_pairs={{0,1},{1,2},{2,3},{3,4},{4,5},{5,6},{6,7},{7,8},{8,9},{9,10},{10,1... | collective-permute-start | bytes 3176 | tf_op jit(solution)/shard_map/ppermute | solution.py:18
  341.3 13.8 %collective-permute-start.46 = (f32[2,2,66,1]{3,2,1,0:T(8,128)S(1)}, f32[2,2,66,1]{3,2,1,0:T(8,128)S(1)}, u32[]{:S(2)}, u32[]{:S(2)}) collective-permute-start(f32[2,2,66,1]{3,2,1,0:T(8,128)S(1)} %get-tuple-element.15), channel_id=1, source_target_pairs={{1,0},{2,1},{3,2},{4,3},{5,4},{6,5},{7,6},{8,7},{9,8},{10,9},{11,1... | collective-permute-start | bytes 3176 | tf_op jit(solution)/shard_map/ppermute | solution.py:18
  355.5 9.8 %collective-permute-start.48 = (f32[2,2,1,256]{3,2,1,0:T(1,128)S(1)}, f32[2,2,1,256]{3,2,1,0:T(1,128)S(1)}, u32[]{:S(2)}, u32[]{:S(2)}) collective-permute-start(f32[2,2,1,256]{3,2,1,0:T(1,128)S(1)} %get-tuple-element.46), channel_id=1, source_target_pairs={{8,0},{9,1},{10,2},{11,3},{12,4},{13,5},{14,6},{15,7},{16,8},{17,9... | collective-permute-start | bytes 12296 | tf_op jit(solution)/shard_map/ppermute | solution.py:18
  357.5 10.3 %collective-permute-start.49 = (f32[2,2,1,256]{3,2,1,0:T(1,128)S(1)}, f32[2,2,1,256]{3,2,1,0:T(1,128)S(1)}, u32[]{:S(2)}, u32[]{:S(2)}) collective-permute-start(f32[2,2,1,256]{3,2,1,0:T(1,128)S(1)} %get-tuple-element.45), channel_id=1, source_target_pairs={{0,8},{1,9},{2,10},{3,11},{4,12},{5,13},{6,14},{7,15},{8,16},{9,17... | collective-permute-start | bytes 12296 | tf_op jit(solution)/shard_map/ppermute | solution.py:18
  368.0 14.2 %collective-permute-start.51 = (f32[2,2,66,1]{3,2,1,0:T(8,128)S(1)}, f32[2,2,66,1]{3,2,1,0:T(8,128)S(1)}, u32[]{:S(2)}, u32[]{:S(2)}) collective-permute-start(f32[2,2,66,1]{3,2,1,0:T(8,128)S(1)} %get-tuple-element.14), channel_id=1, source_target_pairs={{0,1},{1,2},{2,3},{3,4},{4,5},{5,6},{6,7},{7,8},{8,9},{9,10},{10,1... | collective-permute-start | bytes 3176 | tf_op jit(solution)/shard_map/ppermute | solution.py:18
  369.9 13.8 %collective-permute-start.50 = (f32[2,2,66,1]{3,2,1,0:T(8,128)S(1)}, f32[2,2,66,1]{3,2,1,0:T(8,128)S(1)}, u32[]{:S(2)}, u32[]{:S(2)}) collective-permute-start(f32[2,2,66,1]{3,2,1,0:T(8,128)S(1)} %get-tuple-element.13), channel_id=1, source_target_pairs={{1,0},{2,1},{3,2},{4,3},{5,4},{6,5},{7,6},{8,7},{9,8},{10,9},{11,1... | collective-permute-start | bytes 3176 | tf_op jit(solution)/shard_map/ppermute | solution.py:18
  386.1 10.3 %collective-permute-start.53 = (f32[2,2,1,256]{3,2,1,0:T(1,128)S(1)}, f32[2,2,1,256]{3,2,1,0:T(1,128)S(1)}, u32[]{:S(2)}, u32[]{:S(2)}) collective-permute-start(f32[2,2,1,256]{3,2,1,0:T(1,128)S(1)} %get-tuple-element.43), channel_id=1, source_target_pairs={{0,8},{1,9},{2,10},{3,11},{4,12},{5,13},{6,14},{7,15},{8,16},{9,17... | collective-permute-start | bytes 12296 | tf_op jit(solution)/shard_map/ppermute | solution.py:18
  396.6 14.2 %collective-permute-start.55 = (f32[2,2,66,1]{3,2,1,0:T(8,128)S(1)}, f32[2,2,66,1]{3,2,1,0:T(8,128)S(1)}, u32[]{:S(2)}, u32[]{:S(2)}) collective-permute-start(f32[2,2,66,1]{3,2,1,0:T(8,128)S(1)} %get-tuple-element.12), channel_id=1, source_target_pairs={{0,1},{1,2},{2,3},{3,4},{4,5},{5,6},{6,7},{7,8},{8,9},{9,10},{10,1... | collective-permute-start | bytes 3176 | tf_op jit(solution)/shard_map/ppermute | solution.py:18
  398.5 13.8 %collective-permute-start.54 = (f32[2,2,66,1]{3,2,1,0:T(8,128)S(1)}, f32[2,2,66,1]{3,2,1,0:T(8,128)S(1)}, u32[]{:S(2)}, u32[]{:S(2)}) collective-permute-start(f32[2,2,66,1]{3,2,1,0:T(8,128)S(1)} %get-tuple-element.11), channel_id=1, source_target_pairs={{1,0},{2,1},{3,2},{4,3},{5,4},{6,5},{7,6},{8,7},{9,8},{10,9},{11,1... | collective-permute-start | bytes 3176 | tf_op jit(solution)/shard_map/ppermute | solution.py:18
  414.8 10.3 %collective-permute-start.57 = (f32[2,2,1,256]{3,2,1,0:T(1,128)S(1)}, f32[2,2,1,256]{3,2,1,0:T(1,128)S(1)}, u32[]{:S(2)}, u32[]{:S(2)}) collective-permute-start(f32[2,2,1,256]{3,2,1,0:T(1,128)S(1)} %get-tuple-element.41), channel_id=1, source_target_pairs={{0,8},{1,9},{2,10},{3,11},{4,12},{5,13},{6,14},{7,15},{8,16},{9,17... | collective-permute-start | bytes 12296 | tf_op jit(solution)/shard_map/ppermute | solution.py:18
  425.2 14.2 %collective-permute-start.59 = (f32[2,2,66,1]{3,2,1,0:T(8,128)S(1)}, f32[2,2,66,1]{3,2,1,0:T(8,128)S(1)}, u32[]{:S(2)}, u32[]{:S(2)}) collective-permute-start(f32[2,2,66,1]{3,2,1,0:T(8,128)S(1)} %get-tuple-element.10), channel_id=1, source_target_pairs={{0,1},{1,2},{2,3},{3,4},{4,5},{5,6},{6,7},{7,8},{8,9},{9,10},{10,1... | collective-permute-start | bytes 3176 | tf_op jit(solution)/shard_map/ppermute | solution.py:18
  427.1 13.8 %collective-permute-start.58 = (f32[2,2,66,1]{3,2,1,0:T(8,128)S(1)}, f32[2,2,66,1]{3,2,1,0:T(8,128)S(1)}, u32[]{:S(2)}, u32[]{:S(2)}) collective-permute-start(f32[2,2,66,1]{3,2,1,0:T(8,128)S(1)} %get-tuple-element.9), channel_id=1, source_target_pairs={{1,0},{2,1},{3,2},{4,3},{5,4},{6,5},{7,6},{8,7},{9,8},{10,9},{11,1... | collective-permute-start | bytes 3176 | tf_op jit(solution)/shard_map/ppermute | solution.py:18
  443.4 10.3 %collective-permute-start.61 = (f32[2,2,1,256]{3,2,1,0:T(1,128)S(1)}, f32[2,2,1,256]{3,2,1,0:T(1,128)S(1)}, u32[]{:S(2)}, u32[]{:S(2)}) collective-permute-start(f32[2,2,1,256]{3,2,1,0:T(1,128)S(1)} %get-tuple-element.39), channel_id=1, source_target_pairs={{0,8},{1,9},{2,10},{3,11},{4,12},{5,13},{6,14},{7,15},{8,16},{9,17... | collective-permute-start | bytes 12296 | tf_op jit(solution)/shard_map/ppermute | solution.py:18
  453.8 14.2 %collective-permute-start.63 = (f32[2,2,66,1]{3,2,1,0:T(8,128)S(1)}, f32[2,2,66,1]{3,2,1,0:T(8,128)S(1)}, u32[]{:S(2)}, u32[]{:S(2)}) collective-permute-start(f32[2,2,66,1]{3,2,1,0:T(8,128)S(1)} %get-tuple-element.8), channel_id=1, source_target_pairs={{0,1},{1,2},{2,3},{3,4},{4,5},{5,6},{6,7},{7,8},{8,9},{9,10},{10,1... | collective-permute-start | bytes 3176 | tf_op jit(solution)/shard_map/ppermute | solution.py:18
  455.8 13.8 %collective-permute-start.62 = (f32[2,2,66,1]{3,2,1,0:T(8,128)S(1)}, f32[2,2,66,1]{3,2,1,0:T(8,128)S(1)}, u32[]{:S(2)}, u32[]{:S(2)}) collective-permute-start(f32[2,2,66,1]{3,2,1,0:T(8,128)S(1)} %get-tuple-element.7), channel_id=1, source_target_pairs={{1,0},{2,1},{3,2},{4,3},{5,4},{6,5},{7,6},{8,7},{9,8},{10,9},{11,1... | collective-permute-start | bytes 3176 | tf_op jit(solution)/shard_map/ppermute | solution.py:18
  472.0 10.3 %collective-permute-start.65 = (f32[2,2,1,256]{3,2,1,0:T(1,128)S(1)}, f32[2,2,1,256]{3,2,1,0:T(1,128)S(1)}, u32[]{:S(2)}, u32[]{:S(2)}) collective-permute-start(f32[2,2,1,256]{3,2,1,0:T(1,128)S(1)} %get-tuple-element.37), channel_id=1, source_target_pairs={{0,8},{1,9},{2,10},{3,11},{4,12},{5,13},{6,14},{7,15},{8,16},{9,17... | collective-permute-start | bytes 12296 | tf_op jit(solution)/shard_map/ppermute | solution.py:18
  482.5 14.2 %collective-permute-start.67 = (f32[2,2,66,1]{3,2,1,0:T(8,128)S(1)}, f32[2,2,66,1]{3,2,1,0:T(8,128)S(1)}, u32[]{:S(2)}, u32[]{:S(2)}) collective-permute-start(f32[2,2,66,1]{3,2,1,0:T(8,128)S(1)} %get-tuple-element.6), channel_id=1, source_target_pairs={{0,1},{1,2},{2,3},{3,4},{4,5},{5,6},{6,7},{7,8},{8,9},{9,10},{10,1... | collective-permute-start | bytes 3176 | tf_op jit(solution)/shard_map/ppermute | solution.py:18
  484.4 13.8 %collective-permute-start.66 = (f32[2,2,66,1]{3,2,1,0:T(8,128)S(1)}, f32[2,2,66,1]{3,2,1,0:T(8,128)S(1)}, u32[]{:S(2)}, u32[]{:S(2)}) collective-permute-start(f32[2,2,66,1]{3,2,1,0:T(8,128)S(1)} %get-tuple-element.5), channel_id=1, source_target_pairs={{1,0},{2,1},{3,2},{4,3},{5,4},{6,5},{7,6},{8,7},{9,8},{10,9},{11,1... | collective-permute-start | bytes 3176 | tf_op jit(solution)/shard_map/ppermute | solution.py:18
  (10 other events, 211.8 us)
Sparse Core Ops, SparseCore 0:
  499.4 153.1 all-reduce.1
where the time goes:
time: 663 us; the launch traced here: 661 us
  starting transfers between devices  380 us (57%)
  waiting for transfers between devices  252 us (38%)
  between operations  14.9 us (2%)
  other arithmetic  10.8 us (2%)
    ppermute x68, starting transfers between devices, passed_along(): return lax.ppermute(block, axis, route)  380 us
    psum x1, waiting for transfers between devices, local(): summed = lax.psum(partial_sum, 'mem')  153 us
    ppermute x68, waiting for transfers between devices, passed_along(): return lax.ppermute(block, axis, route)  99.1 us
  transfers between devices with their start and end apart: 69, of which 49 were waited for; matrix products, arithmetic and copies ran while one was open for 0% of the time, Pallas kernels for 0%

commit v1 on v0

v1 whole, which is shorter than its diff:
```python
import jax
import jax.numpy as jnp
from jax import lax
from jax.experimental import pallas as pl
from jax.experimental.pallas import tpu as pltpu
from jax.sharding import PartitionSpec as P

COL_TILES = 8
SWEEPS = 8
HALO = 2 * SWEEPS
LANES = 128
FIELDS = 4
TALL = 64 + 2 * HALO
RING = FIELDS * (256 + 2 * HALO)
GROUPS = TALL // 8

ens_weight = 0.7
static_weight = 0.3

F32 = jnp.float32


def masked_coefs(dif_ref, edge_ref):
    nrows, ncols = dif_ref.shape[-2:]
    row = lax.broadcasted_iota(jnp.int32, (nrows, ncols), 0)
    col = lax.broadcasted_iota(jnp.int32, (nrows, ncols), 1)
    row_coef = jnp.where((row == nrows - 1) & (edge_ref[0] == 1), F32(0.0), dif_ref[0])
    col_coef = jnp.where((col == ncols - 1) & (edge_ref[1] == 1), F32(0.0), dif_ref[1])
    return row_coef, col_coef


def own_fields(vec_ref, ens_ref, dif_ref, weight_ref, edge_ref):
    starts = []
    for m in range(2):
        for c in range(2):
            starts.append(weight_ref[...] * ens_ref[m, c].astype(F32) * vec_ref[c])
    return starts + list(masked_coefs(dif_ref, edge_ref))


def row_messages(edge_ref, vec_ref, ens_ref, dif_ref, weight_ref, first_ref, last_ref):
    for k, field in enumerate(own_fields(vec_ref, ens_ref, dif_ref, weight_ref, edge_ref)):
        first_ref[k] = field[:HALO]
        last_ref[k] = field[-HALO:]


def tall_fields(edge_ref, vec_ref, ens_ref, dif_ref, weight_ref, above_ref, below_ref):
    own = own_fields(vec_ref, ens_ref, dif_ref, weight_ref, edge_ref)
    return [jnp.concatenate([above_ref[k], own[k], below_ref[k]], 0) for k in range(6)]


def col_messages(edge_ref, vec_ref, ens_ref, dif_ref, weight_ref, above_ref, below_ref, first_ref, last_ref):
    tall = tall_fields(edge_ref, vec_ref, ens_ref, dif_ref, weight_ref, above_ref, below_ref)
    lane = lax.broadcasted_iota(jnp.int32, (TALL, LANES), 1)
    first = tall[0][:, :LANES]
    last = pltpu.roll(tall[0][:, -LANES:], HALO, 1)
    for k in range(1, 6):
        here = lane >= k * HALO
        first = jnp.where(here, pltpu.roll(tall[k][:, :LANES], k * HALO, 1), first)
        last = jnp.where(here, pltpu.roll(tall[k][:, -LANES:], (k + 1) * HALO, 1), last)
    first_ref[...] = first
    last_ref[...] = last


def sweep(src, dst, row_ref, col_ref, begin, end):
    sub = lax.broadcasted_iota(jnp.int32, (8, RING), 0)
    here = src[8 * begin : 8 * begin + 8, :]
    here_up = pltpu.roll(here, 7, 0)
    flux_above = jnp.zeros((8, RING), F32)
    for g in range(begin, end):
        rows = slice(8 * g, 8 * g + 8)
        if g + 1 < GROUPS:
            after = src[8 * g + 8 : 8 * g + 16, :]
            after_up = pltpu.roll(after, 7, 0)
        else:
            after, after_up = here, here_up
        south = jnp.where(sub == 7, after_up, here_up)
        row_flux = row_ref[rows, :] * (south - here)
        flux_down = pltpu.roll(row_flux, 1, 0)
        north_flux = jnp.where(sub == 0, flux_above, flux_down)
        col_flux = col_ref[rows, :] * (pltpu.roll(here, RING - 1, 1) - here)
        west_flux = pltpu.roll(col_flux, 1, 1)
        dst[rows, :] = here + (row_flux - north_flux) + (col_flux - west_flux)
        here, here_up, flux_above = after, after_up, flux_down


def localize(
    edge_ref, vec_ref, ens_ref, dif_ref, weight_ref, above_ref, below_ref, left_ref, right_ref,
    out_ref, a_ref, b_ref, row_ref, col_ref,
):
    tall = tall_fields(edge_ref, vec_ref, ens_ref, dif_ref, weight_ref, above_ref, below_ref)
    lane = lax.broadcasted_iota(jnp.int32, (TALL, LANES), 1)

    def padded(k):
        right = pltpu.roll(right_ref[...], (LANES - k * HALO) % LANES, 1) if k else right_ref[...]
        left = pltpu.roll(left_ref[...], LANES - (k + 1) * HALO, 1)
        edge = jnp.where(lane < HALO, right, jnp.where(lane >= LANES - HALO, left, F32(0.0)))
        return jnp.concatenate([tall[k], edge], 1)

    def lay(ref, parts):
        for f in range(FIELDS):
            part = parts[f] if f == 0 else pltpu.roll(parts[f], 32 * f, 1)
            base = 256 * f
            if f == 0:
                ref[:, :384] = part
                wrap = part[:, 256:]
            else:
                keep = lane < 32 * f - HALO
                ref[:, base : base + LANES] = jnp.where(keep, tail, part[:, :LANES])
                ref[:, base + LANES : base + 256] = part[:, LANES:256]
            tail = part[:, 256:]
        ref[:, RING - LANES :] = jnp.where(lane < LANES - HALO, tail, wrap)

    lay(a_ref, [padded(f) for f in range(FIELDS)])
    lay(row_ref, [padded(4)] * FIELDS)
    lay(col_ref, [padded(5)] * FIELDS)

    def two(begin, end):
        def body(_, carry):
            sweep(a_ref, b_ref, row_ref, col_ref, begin, end)
            sweep(b_ref, a_ref, row_ref, col_ref, begin, end)
            return carry
        return body

    b_ref[...] = jnp.zeros_like(b_ref)
    lax.fori_loop(0, SWEEPS // 2, two(0, GROUPS), 0)
    lax.fori_loop(0, SWEEPS // 2, two(1, GROUPS - 1), 0)

    for c in range(2):
        total = None
        for m in range(2):
            f = 2 * m + c
            spread = a_ref[HALO:-HALO, 256 * f : 256 * f + 384]
            if f:
                spread = pltpu.roll(spread, 384 - 32 * f, 1)
            term = ens_ref[m, c].astype(F32) * weight_ref[...] * spread[:, :256]
            total = term if total is None else total + term
        for x in range(4):
            out_ref[x, c] = total[16 * x : 16 * x + 16]


def local(vector, ensemble, diffusivity, norm_weight, static_var):
    vec = vector[:, 0]
    weight = norm_weight[0]
    ens = ensemble[:, :, 0]
    dif = diffusivity[:, 0]
    tiles = lax.axis_size("tile")
    row_tiles = tiles // COL_TILES
    tile_id = lax.axis_index("tile")
    edge = jnp.stack(
        [tile_id // COL_TILES == row_tiles - 1, tile_id % COL_TILES == COL_TILES - 1]
    ).astype(jnp.int32)
    vmem = pl.BlockSpec(memory_space=pltpu.VMEM)
    smem = pl.BlockSpec(memory_space=pltpu.SMEM)
    params = pltpu.CompilerParams(vmem_limit_bytes=32 * 2**20)
    own = (edge, vec, ens, dif, weight)
    own_specs = [smem] + [vmem] * 4

    row_msg = jax.ShapeDtypeStruct((6, HALO, 256), F32)
    first, last = pl.pallas_call(
        row_messages, out_shape=(row_msg, row_msg), in_specs=own_specs, out_specs=(vmem, vmem),
        compiler_params=params,
    )(*own)
    down = [(i, i + COL_TILES) for i in range(tiles - COL_TILES)]
    up = [(b, a) for a, b in down]
    above = lax.ppermute(last, "tile", down)
    below = lax.ppermute(first, "tile", up)

    col_msg = jax.ShapeDtypeStruct((TALL, LANES), F32)
    first, last = pl.pallas_call(
        col_messages, out_shape=(col_msg, col_msg), in_specs=own_specs + [vmem] * 2, out_specs=(vmem, vmem),
        compiler_params=params,
    )(*own, above, below)
    rightward = [(i, i + 1) for i in range(tiles) if (i + 1) % COL_TILES]
    leftward = [(b, a) for a, b in rightward]
    left = lax.ppermute(last, "tile", rightward)
    right = lax.ppermute(first, "tile", leftward)

    partial = pl.pallas_call(
        localize,
        out_shape=jax.ShapeDtypeStruct((4, 2, 16, 256), F32),
        in_specs=own_specs + [vmem] * 4,
        out_specs=vmem,
        scratch_shapes=[pltpu.VMEM((TALL, RING), F32)] * 4,
        compiler_params=params,
    )(*own, above, below, left, right)

    along_x = [[0, 1, 2, 3], [4, 5, 6, 7]]
    parts = lax.all_to_all(partial, "mem", 0, 0, axis_index_groups=along_x, tiled=True)
    mine = jnp.sum(parts, 0)
    other = lax.ppermute(mine, "mem", [(i, (i + 4) % 8) for i in range(8)])
    both = jnp.broadcast_to((mine + other)[None], (4, 2, 16, 256))
    summed = lax.all_to_all(both, "mem", 0, 0, axis_index_groups=along_x, tiled=True)
    summed = jnp.swapaxes(summed, 0, 1).reshape(2, 64, 256)
    members = lax.axis_size("mem") * ensemble.shape[0]
    ens_part = summed / F32(members - 1)
    result = ens_weight * ens_part + static_weight * static_var[:, 0] * vec
    return result[:, None]


def solution(mesh):
    placed = (
        P(None, "tile", None, None),
        P("mem", None, "tile", None, None),
        P(None, "tile", None, None),
        P("tile", None, None),
        P(None, "tile", None, None),
    )
    return jax.shard_map(
        local, mesh=mesh, in_specs=placed, out_specs=P(None, "tile", None, None), check_vma=False
    )
```

time: 663 us -> 86.9 us (0.13)
  the two profiles are of different devices: /device:TPU:16 before, /device:TPU:8 now
where the time goes in v1:
time: 86.9 us; the launch traced here: 86.5 us
  starting transfers between devices  28.9 us (33%)
  waiting for transfers between devices  19.8 us (23%)
  blocking collectives  18.4 us (21%)
  Pallas kernels  13.9 us (16%)
  local copies, waits for them, and re-layouts  4.51 us (5%)
    ppermute x1, starting transfers between devices, local(): other = lax.ppermute(mine, 'mem', [(i, (i + 4) % 8) for i in range(8)])  15.2 us
    ppermute x1, waiting for transfers between devices, local(): above = lax.ppermute(last, 'tile', down)  14 us
    pallas_call x1, Pallas kernels, local(): pl.pallas_call(localize, out_shape=jax.ShapeDtypeStruct((4, 2, 16, 256),...  12.6 us
    all_to_all x1, blocking collectives, local(): lax.all_to_all(partial, 'mem', 0, 0, axis_index_groups=along_x, tiled=True)  10.1 us
    ppermute x1, starting transfers between devices, local(): above = lax.ppermute(last, 'tile', down)  9.1 us
    all_to_all x1, blocking collectives, local(): lax.all_to_all(both, 'mem', 0, 0, axis_index_groups=along_x, tiled=True)  8.36 us
    unnamed x12, local copies, waits for them, and re-layouts  4.5 us
    ppermute x1, waiting for transfers between devices, local(): other = lax.ppermute(mine, 'mem', [(i, (i + 4) % 8) for i in range(8)])  2.39 us
  transfers between devices with their start and end apart: 5, of which 4 were waited for; matrix products, arithmetic and copies ran while one was open for 0% of the time, Pallas kernels for 0%

profile of v1, /device:TPU:8, one launch (start us, length us, event | category | flops | bytes accessed | tf_op | source)
XLA Modules:
  0.0 86.5 jit_solution(9156956963764168518)
XLA Ops:
  0.0 0.1 add_convert_fusion.edge_ref
  0.1 0.0 copy-start
  0.1 0.9 %copy-done = f32[2,1,64,256]{3,2,1,0:T(8,128)S(1)} copy-done((f32[2,1,64,256]{3,2,1,0:T(8,128)S(1)}, f32[2,1,64,256]{3,2,1,0:T(8,128)}, u32[]{:S(2)}) %copy-start) | copy-done | bytes 131096
  1.0 0.0 copy-start.2
  1.0 0.9 %copy-done.2 = bf16[2,2,1,64,256]{4,3,2,1,0:T(8,128)(2,1)S(1)} copy-done((bf16[2,2,1,64,256]{4,3,2,1,0:T(8,128)(2,1)S(1)}, bf16[2,2,1,64,256]{4,3,2,1,0:T(8,128)(2,1)}, u32[]{:S(2)}) %copy-start.2) | copy-done | bytes 131096
  1.9 0.0 copy-start.3
  1.9 0.9 %copy-done.3 = f32[2,1,64,256]{3,2,1,0:T(8,128)S(1)} copy-done((f32[2,1,64,256]{3,2,1,0:T(8,128)S(1)}, f32[2,1,64,256]{3,2,1,0:T(8,128)}, u32[]{:S(2)}) %copy-start.3) | copy-done | bytes 131096
  2.8 0.0 copy-start.4
  2.8 0.8 copy-done.4
  3.6 0.6 shard_map.55
  4.2 9.1 %collective-permute-start = (f32[6,16,256]{2,1,0:T(8,128)S(1)}, f32[6,16,256]{2,1,0:T(8,128)S(1)}, u32[]{:S(2)}, u32[]{:S(2)}) collective-permute-start(f32[6,16,256]{2,1,0:T(8,128)S(1)} %get-tuple-element.9), channel_id=1, source_target_pairs={{0,8},{1,9},{2,10},{3,11},{4,12},{5,13},{6,14},{7,15},{8,16},{9,17... | collective-permute-start | bytes 294920 | tf_op jit(solution)/shard_map/ppermute | solution.py:165
  13.3 1.9 %collective-permute-start.1 = (f32[6,16,256]{2,1,0:T(8,128)S(1)}, f32[6,16,256]{2,1,0:T(8,128)S(1)}, u32[]{:S(2)}, u32[]{:S(2)}) collective-permute-start(f32[6,16,256]{2,1,0:T(8,128)S(1)} %get-tuple-element.10), channel_id=1, source_target_pairs={{8,0},{9,1},{10,2},{11,3},{12,4},{13,5},{14,6},{15,7},{16,8},{17,9... | collective-permute-start | bytes 294920 | tf_op jit(solution)/shard_map/ppermute | solution.py:166
  15.2 14.0 %collective-permute-done.above_ref = f32[6,16,256]{2,1,0:T(8,128)S(1)} collective-permute-done((f32[6,16,256]{2,1,0:T(8,128)S(1)}, f32[6,16,256]{2,1,0:T(8,128)S(1)}, u32[]{:S(2)}, u32[]{:S(2)}) %collective-permute-start) | collective-permute-done | bytes 98336 | tf_op jit(solution)/shard_map/ppermute | solution.py:165
  29.2 1.6 %collective-permute-done.1.below_ref = f32[6,16,256]{2,1,0:T(8,128)S(1)} collective-permute-done((f32[6,16,256]{2,1,0:T(8,128)S(1)}, f32[6,16,256]{2,1,0:T(8,128)S(1)}, u32[]{:S(2)}, u32[]{:S(2)}) %collective-permute-start.1) | collective-permute-done | bytes 98336 | tf_op jit(solution)/shard_map/ppermute | solution.py:166
  30.8 0.7 shard_map.56
  31.6 1.4 %collective-permute-start.2 = (f32[96,128]{1,0:T(8,128)S(1)}, f32[96,128]{1,0:T(8,128)S(1)}, u32[]{:S(2)}, u32[]{:S(2)}) collective-permute-start(f32[96,128]{1,0:T(8,128)S(1)} %get-tuple-element.11), channel_id=1, source_target_pairs={{0,1},{1,2},{2,3},{3,4},{4,5},{5,6},{6,7},{8,9},{9,10},{10,11},{11... | collective-permute-start | bytes 147464 | tf_op jit(solution)/shard_map/ppermute | solution.py:175
  33.0 1.3 %collective-permute-start.3 = (f32[96,128]{1,0:T(8,128)S(1)}, f32[96,128]{1,0:T(8,128)S(1)}, u32[]{:S(2)}, u32[]{:S(2)}) collective-permute-start(f32[96,128]{1,0:T(8,128)S(1)} %get-tuple-element.12), channel_id=1, source_target_pairs={{1,0},{2,1},{3,2},{4,3},{5,4},{6,5},{7,6},{9,8},{10,9},{11,10},{12... | collective-permute-start | bytes 147464 | tf_op jit(solution)/shard_map/ppermute | solution.py:176
  34.3 0.0 collective-permute-done.2.left_ref
  34.3 1.8 %collective-permute-done.3.right_ref = f32[96,128]{1,0:T(8,128)S(1)} collective-permute-done((f32[96,128]{1,0:T(8,128)S(1)}, f32[96,128]{1,0:T(8,128)S(1)}, u32[]{:S(2)}, u32[]{:S(2)}) %collective-permute-start.3) | collective-permute-done | bytes 49184 | tf_op jit(solution)/shard_map/ppermute | solution.py:176
  36.1 12.6 %shard_map.57 = f32[4,2,16,256]{3,2,1,0:T(8,128)S(1)} custom-call(s32[2]{0:T(128)S(1)} %add_convert_fusion.edge_ref, f32[2,64,256]{2,1,0:T(8,128)S(1)} %bitcast.23, bf16[2,2,64,256]{3,2,1,0:T(8,128)(2,1)S(1)} %bitcast.26, f32[2,64,256]{2,1,0:T(8,128)S(1)} %bitcast.29, f32[64,256]{1,0:T(8,128)S(1)} %bitcast.32, ...), custom_call_target="tpu_custom_call" | custom-call | tf_op jit(solution)/shard_map/pallas_call | solution.py:178
  48.8 10.1 %all_to_all.10 = f32[4,2,16,256]{3,2,1,0:T(8,128)S(1)} all-to-all(f32[4,2,16,256]{3,2,1,0:T(8,128)S(1)} %shard_map.57), channel_id=1, replica_groups={{0,64,128,192},{256,320,384,448},{1,65,129,193},{257,321,385,449},{2,66..., dimensions={0} | all-to-all | bytes 262144 | tf_op jit(solution)/shard_map/all_to_all | solution.py:188
  58.9 15.2 %collective-permute-start.4 = (f32[2,16,256]{2,1,0:T(8,128)S(1)}, f32[2,16,256]{2,1,0:T(8,128)S(1)}, u32[]{:S(2)}, u32[]{:S(2)}) collective-permute-start(f32[2,16,256]{2,1,0:T(8,128)S(1)} %reduce_sum.9), channel_id=1, source_target_pairs={{0,256},{64,320},{128,384},{192,448},{256,0},{320,64},{384,128},{4... | collective-permute-start | bytes 98312 | tf_op jit(solution)/shard_map/ppermute | solution.py:190
  74.1 2.4 %collective-permute-done.4 = f32[2,16,256]{2,1,0:T(8,128)S(1)} collective-permute-done((f32[2,16,256]{2,1,0:T(8,128)S(1)}, f32[2,16,256]{2,1,0:T(8,128)S(1)}, u32[]{:S(2)}, u32[]{:S(2)}) %collective-permute-start.4) | collective-permute-done | bytes 32800 | tf_op jit(solution)/shard_map/ppermute | solution.py:190
  76.5 8.4 %all_to_all.11 = f32[4,2,16,256]{3,2,1,0:T(8,128)S(1)} all-to-all(f32[4,2,16,256]{3,2,1,0:T(8,128)S(1)} %broadcast_in_dim.2), channel_id=1, replica_groups={{0,64,128,192},{256,320,384,448},{1,65,129,193},{257,321,385,449},{2,66..., dimensions={0} | all-to-all | bytes 262144 | tf_op jit(solution)/shard_map/all_to_all | solution.py:192
  84.9 0.0 copy-start.1
  84.9 0.0 copy-start.5
  84.9 0.9 %copy-done.1 = f32[2,1,64,256]{3,2,1,0:T(8,128)S(1)} copy-done((f32[2,1,64,256]{3,2,1,0:T(8,128)S(1)}, f32[2,1,64,256]{3,2,1,0:T(8,128)}, u32[]{:S(2)}) %copy-start.1) | copy-done | bytes 131096
  85.8 0.1 copy-done.5
  85.8 0.7 fusion.1
  (4 shorter events, 0.0 us)
Async XLA Ops:
  0.1 0.9 %copy-start = (f32[2,1,64,256]{3,2,1,0:T(8,128)S(1)}, f32[2,1,64,256]{3,2,1,0:T(8,128)}, u32[]{:S(2)}) copy-start(f32[2,1,64,256]{3,2,1,0:T(8,128)} %param.5) | copy-start | bytes 393220
  1.0 0.9 %copy-start.2 = (bf16[2,2,1,64,256]{4,3,2,1,0:T(8,128)(2,1)S(1)}, bf16[2,2,1,64,256]{4,3,2,1,0:T(8,128)(2,1)}, u32[]{:S(2)}) copy-start(bf16[2,2,1,64,256]{4,3,2,1,0:T(8,128)(2,1)} %param.6) | copy-start | bytes 393220
  1.9 0.9 %copy-start.3 = (f32[2,1,64,256]{3,2,1,0:T(8,128)S(1)}, f32[2,1,64,256]{3,2,1,0:T(8,128)}, u32[]{:S(2)}) copy-start(f32[2,1,64,256]{3,2,1,0:T(8,128)} %param.7) | copy-start | bytes 393220
  2.8 0.8 copy-start.4
  4.2 25.0 %collective-permute-start = (f32[6,16,256]{2,1,0:T(8,128)S(1)}, f32[6,16,256]{2,1,0:T(8,128)S(1)}, u32[]{:S(2)}, u32[]{:S(2)}) collective-permute-start(f32[6,16,256]{2,1,0:T(8,128)S(1)} %get-tuple-element.9), channel_id=1, source_target_pairs={{0,8},{1,9},{2,10},{3,11},{4,12},{5,13},{6,14},{7,15},{8,16},{9,17... | collective-permute-start | bytes 294920 | tf_op jit(solution)/shard_map/ppermute | solution.py:165
  13.3 17.5 %collective-permute-start.1 = (f32[6,16,256]{2,1,0:T(8,128)S(1)}, f32[6,16,256]{2,1,0:T(8,128)S(1)}, u32[]{:S(2)}, u32[]{:S(2)}) collective-permute-start(f32[6,16,256]{2,1,0:T(8,128)S(1)} %get-tuple-element.10), channel_id=1, source_target_pairs={{8,0},{9,1},{10,2},{11,3},{12,4},{13,5},{14,6},{15,7},{16,8},{17,9... | collective-permute-start | bytes 294920 | tf_op jit(solution)/shard_map/ppermute | solution.py:166
  31.6 2.7 %collective-permute-start.2 = (f32[96,128]{1,0:T(8,128)S(1)}, f32[96,128]{1,0:T(8,128)S(1)}, u32[]{:S(2)}, u32[]{:S(2)}) collective-permute-start(f32[96,128]{1,0:T(8,128)S(1)} %get-tuple-element.11), channel_id=1, source_target_pairs={{0,1},{1,2},{2,3},{3,4},{4,5},{5,6},{6,7},{8,9},{9,10},{10,11},{11... | collective-permute-start | bytes 147464 | tf_op jit(solution)/shard_map/ppermute | solution.py:175
  33.0 3.1 %collective-permute-start.3 = (f32[96,128]{1,0:T(8,128)S(1)}, f32[96,128]{1,0:T(8,128)S(1)}, u32[]{:S(2)}, u32[]{:S(2)}) collective-permute-start(f32[96,128]{1,0:T(8,128)S(1)} %get-tuple-element.12), channel_id=1, source_target_pairs={{1,0},{2,1},{3,2},{4,3},{5,4},{6,5},{7,6},{9,8},{10,9},{11,10},{12... | collective-permute-start | bytes 147464 | tf_op jit(solution)/shard_map/ppermute | solution.py:176
  58.9 17.6 %collective-permute-start.4 = (f32[2,16,256]{2,1,0:T(8,128)S(1)}, f32[2,16,256]{2,1,0:T(8,128)S(1)}, u32[]{:S(2)}, u32[]{:S(2)}) collective-permute-start(f32[2,16,256]{2,1,0:T(8,128)S(1)} %reduce_sum.9), channel_id=1, source_target_pairs={{0,256},{64,320},{128,384},{192,448},{256,0},{320,64},{384,128},{4... | collective-permute-start | bytes 98312 | tf_op jit(solution)/shard_map/ppermute | solution.py:190
  84.9 0.9 %copy-start.1 = (f32[2,1,64,256]{3,2,1,0:T(8,128)S(1)}, f32[2,1,64,256]{3,2,1,0:T(8,128)}, u32[]{:S(2)}) copy-start(f32[2,1,64,256]{3,2,1,0:T(8,128)} %param.5) | copy-start | bytes 393220
  84.9 1.0 %copy-start.5 = (f32[2,1,64,256]{3,2,1,0:T(8,128)S(1)}, f32[2,1,64,256]{3,2,1,0:T(8,128)}, u32[]{:S(2)}) copy-start(f32[2,1,64,256]{3,2,1,0:T(8,128)} %param.9) | copy-start | bytes 393220

commit v2 on v1

v2 whole, which is shorter than its diff:
```python
import jax
import jax.numpy as jnp
from jax import lax
from jax.experimental import pallas as pl
from jax.experimental.pallas import tpu as pltpu
from jax.sharding import PartitionSpec as P

COL_TILES = 8
SWEEPS = 8
HALO = 2 * SWEEPS
LANES = 128
FIELDS = 4
TALL = 64 + 2 * HALO
RING = FIELDS * (256 + 2 * HALO)
GROUPS = TALL // 8

ens_weight = 0.7
static_weight = 0.3

F32 = jnp.float32


def fetch(pairs, sems):
    copies = [pltpu.make_async_copy(src, dst, sems.at[i]) for i, (src, dst) in enumerate(pairs)]
    for copy in copies:
        copy.start()
    for copy in copies:
        copy.wait()


def row_messages(edge_ref, vec_hbm, ens_hbm, dif_hbm, weight_hbm, first_ref, last_ref, vec, ens, dif, weight, sems):
    nrows = vec_hbm.shape[2]
    pairs = []
    for side, begin in enumerate((0, nrows - HALO)):
        rows = pl.ds(begin, HALO)
        pairs += [
            (vec_hbm.at[:, 0, rows, :], vec.at[side]),
            (ens_hbm.at[:, :, 0, rows, :], ens.at[side]),
            (dif_hbm.at[:, 0, rows, :], dif.at[side]),
            (weight_hbm.at[0, rows, :], weight.at[side]),
        ]
    fetch(pairs, sems)
    row = lax.broadcasted_iota(jnp.int32, (HALO, 256), 0)
    col = lax.broadcasted_iota(jnp.int32, (HALO, 256), 1)
    for side, ref in enumerate((first_ref, last_ref)):
        for m in range(2):
            for c in range(2):
                ref[2 * m + c] = weight[side] * ens[side, m, c].astype(F32) * vec[side, c]
        row_coef, col_coef = dif[side, 0], dif[side, 1]
        if side == 1:
            row_coef = jnp.where((row == HALO - 1) & (edge_ref[0] == 1), F32(0.0), row_coef)
        ref[4] = row_coef
        ref[5] = jnp.where((col == 255) & (edge_ref[1] == 1), F32(0.0), col_coef)


def pack_cols(fields):
    lane = lax.broadcasted_iota(jnp.int32, (fields[0].shape[0], LANES), 1)
    first = fields[0][:, :LANES]
    last = pltpu.roll(fields[0][:, -LANES:], HALO, 1)
    for k in range(1, 6):
        here = lane >= k * HALO
        first = jnp.where(here, pltpu.roll(fields[k][:, :LANES], k * HALO, 1), first)
        last = jnp.where(here, pltpu.roll(fields[k][:, -LANES:], (k + 1) * HALO, 1), last)
    return first, last


def own_arrays(
    edge_ref, vec_hbm, ens_hbm, dif_hbm, weight_hbm, var_hbm, sent_hbm,
    own_ref, scale_ref, fixed_ref, first_ref, last_ref, vec, ens, dif, weight, var, sems,
):
    fetch(
        [
            (vec_hbm.at[:, 0], vec), (ens_hbm.at[:, :, 0], ens), (dif_hbm.at[:, 0], dif),
            (weight_hbm.at[0], weight), (var_hbm.at[:, 0], var),
        ],
        sems,
    )
    nrows, ncols = weight.shape
    for m in range(2):
        for c in range(2):
            scale = weight[...] * ens[m, c].astype(F32)
            scale_ref[2 * m + c] = scale
            own_ref[2 * m + c] = scale * vec[c]
    row = lax.broadcasted_iota(jnp.int32, (nrows, ncols), 0)
    col = lax.broadcasted_iota(jnp.int32, (nrows, ncols), 1)
    own_ref[4] = jnp.where((row == nrows - 1) & (edge_ref[0] == 1), F32(0.0), dif[0])
    own_ref[5] = jnp.where((col == ncols - 1) & (edge_ref[1] == 1), F32(0.0), dif[1])
    for c in range(2):
        fixed_ref[c] = F32(static_weight) * var[c] * vec[c]
    first_ref[...], last_ref[...] = pack_cols([own_ref[k] for k in range(6)])


def col_messages(first_own, last_own, above_ref, below_ref, first_ref, last_ref):
    for rows, ref in ((slice(0, HALO), above_ref), (slice(TALL - HALO, TALL), below_ref)):
        first_ref[rows, :], last_ref[rows, :] = pack_cols([ref[k] for k in range(6)])
    first_ref[HALO:-HALO, :] = first_own[...]
    last_ref[HALO:-HALO, :] = last_own[...]


PAD = 8
COLUMNS = RING // LANES


def sweep(src, dst, row_ref, col_ref, west_ref, begin, end):
    lane = lax.broadcasted_iota(jnp.int32, (8, LANES), 1)

    def turned(g):
        p = PAD + 8 * g
        here = [src[j, p : p + 8, :] for j in range(COLUMNS)]
        return here, [pltpu.roll(x, LANES - 1, 1) for x in here], [pltpu.roll(x, 1, 1) for x in here]

    ready = turned(begin)
    for g in range(begin, end):
        here, from_east, from_west = ready
        if g + 1 < end:
            ready = turned(g + 1)
        p = PAD + 8 * g
        for j in range(COLUMNS):
            x = here[j]
            east = jnp.where(lane == LANES - 1, from_east[(j + 1) % COLUMNS], from_east[j])
            west = jnp.where(lane == 0, from_west[j - 1], from_west[j])
            south, north = src[j, p + 1 : p + 9, :], src[j, p - 1 : p + 7, :]
            rows = row_ref[j, p : p + 8, :] * (south - x) - row_ref[j, p - 1 : p + 7, :] * (x - north)
            cols = col_ref[j, p : p + 8, :] * (east - x) - west_ref[j, p : p + 8, :] * (x - west)
            dst[j, p : p + 8, :] = x + rows + cols


def localize(
    own_ref, scale_ref, above_ref, below_ref, left_ref, right_ref,
    out_ref, a_ref, b_ref, row_ref, col_ref, west_ref,
):
    lane = lax.broadcasted_iota(jnp.int32, (TALL, LANES), 1)
    tall = slice(PAD, PAD + TALL)

    def padded(k):
        right = pltpu.roll(right_ref[...], (LANES - k * HALO) % LANES, 1) if k else right_ref[...]
        left = pltpu.roll(left_ref[...], LANES - (k + 1) * HALO, 1)
        edge = jnp.where(lane < HALO, right, jnp.where(lane >= LANES - HALO, left, F32(0.0)))
        return jnp.concatenate([jnp.concatenate([above_ref[k], own_ref[k], below_ref[k]], 0), edge], 1)

    def lay(ref, parts):
        for f in range(FIELDS):
            part = pltpu.roll(parts[f], 32 * f, 1) if f else parts[f]
            if f:
                ref[2 * f, tall, :] = jnp.where(lane < 32 * f - HALO, tail, part[:, :LANES])
            else:
                ref[0, tall, :] = part[:, :LANES]
                wrap = part[:, 256:]
            ref[2 * f + 1, tall, :] = part[:, LANES:256]
            tail = part[:, 256:]
        ref[COLUMNS - 1, tall, :] = jnp.where(lane < LANES - HALO, tail, wrap)

    for ref in (a_ref, b_ref, row_ref):
        ref[:, :PAD, :] = jnp.zeros((COLUMNS, PAD, LANES), F32)
        ref[:, PAD + TALL :, :] = jnp.zeros((COLUMNS, PAD, LANES), F32)
    lay(a_ref, [padded(f) for f in range(FIELDS)])
    lay(row_ref, [padded(4)] * FIELDS)
    lay(col_ref, [padded(5)] * FIELDS)
    for j in range(COLUMNS):
        before = pltpu.roll(col_ref[(j - 1) % COLUMNS, tall, :], 1, 1)
        west_ref[j, tall, :] = jnp.where(lane == 0, before, pltpu.roll(col_ref[j, tall, :], 1, 1))

    def two(begin, end):
        def body(_, carry):
            sweep(a_ref, b_ref, row_ref, col_ref, west_ref, begin, end)
            sweep(b_ref, a_ref, row_ref, col_ref, west_ref, begin, end)
            return carry
        return body

    lax.fori_loop(0, SWEEPS // 2, two(0, GROUPS), 0)
    lax.fori_loop(0, SWEEPS // 2, two(1, GROUPS - 1), 0)

    inner = slice(PAD + HALO, PAD + TALL - HALO)
    for c in range(2):
        total = None
        for m in range(2):
            f = 2 * m + c
            spread = jnp.concatenate([a_ref[2 * f + i, inner, :] for i in range(3)], 1)
            if f:
                spread = pltpu.roll(spread, 384 - 32 * f, 1)
            term = scale_ref[f] * spread[:, :256]
            total = term if total is None else total + term
        out_ref[2 * c] = total[:32]
        out_ref[2 * c + 1] = total[32:]


def local(vector, ensemble, diffusivity, norm_weight, static_var):
    tiles = lax.axis_size("tile")
    row_tiles = tiles // COL_TILES
    tile_id = lax.axis_index("tile")
    edge = jnp.stack(
        [tile_id // COL_TILES == row_tiles - 1, tile_id % COL_TILES == COL_TILES - 1]
    ).astype(jnp.int32)
    vmem = pl.BlockSpec(memory_space=pltpu.VMEM)
    smem = pl.BlockSpec(memory_space=pltpu.SMEM)
    hbm = pl.BlockSpec(memory_space=pltpu.HBM)
    params = pltpu.CompilerParams(vmem_limit_bytes=32 * 2**20)

    def f32(*shape):
        return jax.ShapeDtypeStruct(shape, F32)

    def buffers(*lead, rows):
        return [
            pltpu.VMEM((*lead, 2, rows, 256), F32), pltpu.VMEM((*lead, 2, 2, rows, 256), jnp.bfloat16),
            pltpu.VMEM((*lead, 2, rows, 256), F32), pltpu.VMEM((*lead, rows, 256), F32),
        ]

    held = [
        pltpu.with_memory_space_constraint(x, pltpu.HBM)
        for x in (vector, ensemble, diffusivity, norm_weight, static_var)
    ]
    first, last = pl.pallas_call(
        row_messages, out_shape=(f32(6, HALO, 256),) * 2, in_specs=[smem] + [hbm] * 4, out_specs=(vmem,) * 2,
        scratch_shapes=buffers(2, rows=HALO) + [pltpu.SemaphoreType.DMA((8,))],
        compiler_params=params,
    )(edge, *held[:4])
    down = [(i, i + COL_TILES) for i in range(tiles - COL_TILES)]
    up = [(b, a) for a, b in down]
    above = lax.ppermute(last, "tile", down)
    below = lax.ppermute(first, "tile", up)

    own, scale, fixed, first_own, last_own = pl.pallas_call(
        own_arrays,
        out_shape=(f32(6, 64, 256), f32(4, 64, 256), f32(2, 64, 256), f32(64, LANES), f32(64, LANES)),
        in_specs=[smem] + [hbm] * 6, out_specs=(vmem,) * 5,
        scratch_shapes=buffers(rows=64) + [pltpu.VMEM((2, 64, 256), F32), pltpu.SemaphoreType.DMA((5,))],
        compiler_params=params,
        cost_estimate=pl.CostEstimate(flops=2 * 10**6, bytes_accessed=2 * 10**6, transcendentals=0),
    )(edge, *held, first)

    first, last = pl.pallas_call(
        col_messages, out_shape=(f32(TALL, LANES),) * 2, in_specs=[vmem] * 4, out_specs=(vmem,) * 2,
        compiler_params=params,
    )(first_own, last_own, above, below)
    rightward = [(i, i + 1) for i in range(tiles) if (i + 1) % COL_TILES]
    leftward = [(b, a) for a, b in rightward]
    left = lax.ppermute(last, "tile", rightward)
    right = lax.ppermute(first, "tile", leftward)

    partial = pl.pallas_call(
        localize,
        out_shape=f32(4, 32, 256),
        in_specs=[vmem] * 6,
        out_specs=vmem,
        scratch_shapes=[pltpu.VMEM((COLUMNS, TALL + 2 * PAD, LANES), F32)] * 5,
        compiler_params=params,
    )(own, scale, above, below, left, right)

    along_x = [[0, 1, 2, 3], [4, 5, 6, 7]]
    parts = lax.all_to_all(partial, "mem", 0, 0, axis_index_groups=along_x, tiled=True)
    mine = jnp.sum(parts, 0)
    other = lax.ppermute(mine, "mem", [(i, (i + 4) % 8) for i in range(8)])
    both = jnp.broadcast_to((mine + other)[None], (4, 32, 256))
    summed = lax.all_to_all(both, "mem", 0, 0, axis_index_groups=along_x, tiled=True)
    members = lax.axis_size("mem") * ensemble.shape[0]
    ens_part = summed.reshape(2, 64, 256) / F32(members - 1)
    result = ens_weight * ens_part + fixed
    return result[:, None]


def solution(mesh):
    placed = (
        P(None, "tile", None, None),
        P("mem", None, "tile", None, None),
        P(None, "tile", None, None),
        P("tile", None, None),
        P(None, "tile", None, None),
    )
    return jax.shard_map(
        local, mesh=mesh, in_specs=placed, out_specs=P(None, "tile", None, None), check_vma=False
    )
```

time: 86.9 us -> 75 us (0.86)
  Pallas kernels: 13.9 us -> 8.5 us
  local copies, waits for them, and re-layouts: 4.51 us -> 0.01 us
  waiting for transfers between devices: 19.8 us -> 17.9 us
    pallas_call x3 -> x4, Pallas kernels: 13.9 us -> 8.5 us  [the longest x1 5 us: local(): pl.pallas_call(localize, out_shape=f32(4, 32, 256), in_specs=[vmem] * 6,...]
    unnamed x12 -> x0, local copies, waits for them, and re-layouts: 4.5 us -> none
    ppermute x1, waiting for transfers between devices: 14 us -> 12 us  [local(): above = lax.ppermute(last, 'tile', down)]
  transfers between devices with their start and end apart: 5 -> 5, of which waited for: 4 -> 4; matrix products, arithmetic and copies ran while one was open for 0% -> 0% of each run, Pallas kernels for 0% -> 3%
where the time goes in v2:
time: 75 us; the launch traced here: 74.6 us
  starting transfers between devices  28.9 us (39%)
  blocking collectives  18.4 us (25%)
  waiting for transfers between devices  17.9 us (24%)
  Pallas kernels  8.5 us (11%)
  other arithmetic  0.78 us (1%)
    ppermute x1, starting transfers between devices, local(): other = lax.ppermute(mine, 'mem', [(i, (i + 4) % 8) for i in range(8)])  15.2 us
    ppermute x1, waiting for transfers between devices, local(): above = lax.ppermute(last, 'tile', down)  12 us
    all_to_all x1, blocking collectives, local(): lax.all_to_all(partial, 'mem', 0, 0, axis_index_groups=along_x, tiled=True)  10.1 us
    ppermute x1, starting transfers between devices, local(): above = lax.ppermute(last, 'tile', down)  9.1 us
    all_to_all x1, blocking collectives, local(): lax.all_to_all(both, 'mem', 0, 0, axis_index_groups=along_x, tiled=True)  8.36 us
    pallas_call x1, Pallas kernels, local(): pl.pallas_call(localize, out_shape=f32(4, 32, 256), in_specs=[vmem] * 6,...  5 us
    ppermute x1, waiting for transfers between devices, local(): other = lax.ppermute(mine, 'mem', [(i, (i + 4) % 8) for i in range(8)])  2.39 us
    ppermute x1, starting transfers between devices, local(): below = lax.ppermute(first, 'tile', up)  1.92 us
  transfers between devices with their start and end apart: 5, of which 4 were waited for; matrix products, arithmetic and copies ran while one was open for 0% of the time, Pallas kernels for 3%

profile of v2, /device:TPU:8, one launch (start us, length us, event | category | flops | bytes accessed | tf_op | source)
XLA Modules:
  0.0 74.6 jit_solution(1553598789620376315)
XLA Ops:
  0.0 0.1 add_convert_fusion.edge_ref
  0.1 1.5 %shard_map.55 = (f32[6,16,256]{2,1,0:T(8,128)S(1)}, f32[6,16,256]{2,1,0:T(8,128)S(1)}) custom-call(s32[2]{0:T(128)S(1)} %add_convert_fusion.edge_ref, f32[2,1,64,256]{3,2,1,0:T(8,128)} %vec_hbm.3, bf16[2,2,1,64,256]{4,3,2,1,0:T(8,128)(2,1)} %ens_hbm.3, f32[2,1,64,256]{3,2,1,0:T(8,128)} %dif_hbm.3, f32[1,64,256]{2,1,0:T(8,128)} %weight_hbm.3), custom_call_target="tpu_custom_call" | custom-call | tf_op jit(solution)/shard_map/pallas_call | solution.py:212
  1.6 9.1 %collective-permute-start = (f32[6,16,256]{2,1,0:T(8,128)S(1)}, f32[6,16,256]{2,1,0:T(8,128)S(1)}, u32[]{:S(2)}, u32[]{:S(2)}) collective-permute-start(f32[6,16,256]{2,1,0:T(8,128)S(1)} %get-tuple-element.17), channel_id=1, source_target_pairs={{0,8},{1,9},{2,10},{3,11},{4,12},{5,13},{6,14},{7,15},{8,16},{9,17... | collective-permute-start | bytes 294920 | tf_op jit(solution)/shard_map/ppermute | solution.py:219
  10.7 1.9 %collective-permute-start.1 = (f32[6,16,256]{2,1,0:T(8,128)S(1)}, f32[6,16,256]{2,1,0:T(8,128)S(1)}, u32[]{:S(2)}, u32[]{:S(2)}) collective-permute-start(f32[6,16,256]{2,1,0:T(8,128)S(1)} %get-tuple-element.14.sent_hbm), channel_id=1, source_target_pairs={{8,0},{9,1},{10,2},{11,3},{12,4},{13,5},{14,6},{15,7},{16,8},{17,9... | collective-permute-start | bytes 294920 | tf_op jit(solution)/shard_map/ppermute | solution.py:220
  12.6 1.9 %shard_map.56 = (f32[6,64,256]{2,1,0:T(8,128)S(1)}, f32[4,64,256]{2,1,0:T(8,128)S(1)}, f32[2,64,256]{2,1,0:T(8,128)S(1)}, f32[64,128]{1,0:T(8,128)S(1)}, f32[64,128]{1,0:T(8,128)S(1)}) custom-call(s32[2]{0:T(128)S(1)} %add_convert_fusion.edge_ref, f32[2,1,64,256]{3,2,1,0:T(8,128)} %vec_hbm.3, bf16[2,2,1,64,256]{4,3,2,1,0:T(8,128)(2,1)} %ens_hbm.3, ...), custom_call_target="tpu_custom_call" | custom-call | flops 2000000 | bytes 2000000 | tf_op jit(solution)/shard_map/pallas_call | solution.py:222
  14.5 12.0 %collective-permute-done.above_ref = f32[6,16,256]{2,1,0:T(8,128)S(1)} collective-permute-done((f32[6,16,256]{2,1,0:T(8,128)S(1)}, f32[6,16,256]{2,1,0:T(8,128)S(1)}, u32[]{:S(2)}, u32[]{:S(2)}) %collective-permute-start) | collective-permute-done | bytes 98336 | tf_op jit(solution)/shard_map/ppermute | solution.py:219
  26.6 1.6 %collective-permute-done.1.below_ref = f32[6,16,256]{2,1,0:T(8,128)S(1)} collective-permute-done((f32[6,16,256]{2,1,0:T(8,128)S(1)}, f32[6,16,256]{2,1,0:T(8,128)S(1)}, u32[]{:S(2)}, u32[]{:S(2)}) %collective-permute-start.1) | collective-permute-done | bytes 98336 | tf_op jit(solution)/shard_map/ppermute | solution.py:220
  28.2 0.1 shard_map.57
  28.3 1.4 %collective-permute-start.2 = (f32[96,128]{1,0:T(8,128)S(1)}, f32[96,128]{1,0:T(8,128)S(1)}, u32[]{:S(2)}, u32[]{:S(2)}) collective-permute-start(f32[96,128]{1,0:T(8,128)S(1)} %get-tuple-element.20), channel_id=1, source_target_pairs={{0,1},{1,2},{2,3},{3,4},{4,5},{5,6},{6,7},{8,9},{9,10},{10,11},{11... | collective-permute-start | bytes 147464 | tf_op jit(solution)/shard_map/ppermute | solution.py:237
  29.7 1.3 %collective-permute-start.3 = (f32[96,128]{1,0:T(8,128)S(1)}, f32[96,128]{1,0:T(8,128)S(1)}, u32[]{:S(2)}, u32[]{:S(2)}) collective-permute-start(f32[96,128]{1,0:T(8,128)S(1)} %get-tuple-element.21), channel_id=1, source_target_pairs={{1,0},{2,1},{3,2},{4,3},{5,4},{6,5},{7,6},{9,8},{10,9},{11,10},{12... | collective-permute-start | bytes 147464 | tf_op jit(solution)/shard_map/ppermute | solution.py:238
  31.0 0.0 collective-permute-done.2.left_ref
  31.1 1.8 %collective-permute-done.3.right_ref = f32[96,128]{1,0:T(8,128)S(1)} collective-permute-done((f32[96,128]{1,0:T(8,128)S(1)}, f32[96,128]{1,0:T(8,128)S(1)}, u32[]{:S(2)}, u32[]{:S(2)}) %collective-permute-start.3) | collective-permute-done | bytes 49184 | tf_op jit(solution)/shard_map/ppermute | solution.py:238
  32.9 5.0 %shard_map.58 = f32[4,32,256]{2,1,0:T(8,128)S(1)} custom-call(f32[6,64,256]{2,1,0:T(8,128)S(1)} %get-tuple-element.15.own_ref, f32[4,64,256]{2,1,0:T(8,128)S(1)} %get-tuple-element.16.scale_ref, f32[6,16,256]{2,1,0:T(8,128)S(1)} %collective-permute-done.above_ref, f32[6,16,256]{2,1,0:T(8,128)S(1)} %collective-permute-done.1.below_ref, ...), custom_call_target="tpu_custom_call" | custom-call | tf_op jit(solution)/shard_map/pallas_call | solution.py:240
  37.9 10.1 %all_to_all.10 = f32[4,32,256]{2,1,0:T(8,128)S(1)} all-to-all(f32[4,32,256]{2,1,0:T(8,128)S(1)} %shard_map.58), channel_id=1, replica_groups={{0,64,128,192},{256,320,384,448},{1,65,129,193},{257,321,385,449},{2,66..., dimensions={0} | all-to-all | bytes 262144 | tf_op jit(solution)/shard_map/all_to_all | solution.py:250
  48.0 15.2 %collective-permute-start.4 = (f32[32,256]{1,0:T(8,128)S(1)}, f32[32,256]{1,0:T(8,128)S(1)}, u32[]{:S(2)}, u32[]{:S(2)}) collective-permute-start(f32[32,256]{1,0:T(8,128)S(1)} %reduce_sum.9), channel_id=1, source_target_pairs={{0,256},{64,320},{128,384},{192,448},{256,0},{320,64},{384,128},{4... | collective-permute-start | bytes 98312 | tf_op jit(solution)/shard_map/ppermute | solution.py:252
  63.2 2.4 %collective-permute-done.4 = f32[32,256]{1,0:T(8,128)S(1)} collective-permute-done((f32[32,256]{1,0:T(8,128)S(1)}, f32[32,256]{1,0:T(8,128)S(1)}, u32[]{:S(2)}, u32[]{:S(2)}) %collective-permute-start.4) | collective-permute-done | bytes 32800 | tf_op jit(solution)/shard_map/ppermute | solution.py:252
  65.6 8.4 %all_to_all.11 = f32[4,32,256]{2,1,0:T(8,128)S(1)} all-to-all(f32[4,32,256]{2,1,0:T(8,128)S(1)} %broadcast_in_dim.4), channel_id=1, replica_groups={{0,64,128,192},{256,320,384,448},{1,65,129,193},{257,321,385,449},{2,66..., dimensions={0} | all-to-all | bytes 262144 | tf_op jit(solution)/shard_map/all_to_all | solution.py:254
  74.0 0.7 fusion
  (4 shorter events, 0.0 us)
Async XLA Ops:
  1.6 25.0 %collective-permute-start = (f32[6,16,256]{2,1,0:T(8,128)S(1)}, f32[6,16,256]{2,1,0:T(8,128)S(1)}, u32[]{:S(2)}, u32[]{:S(2)}) collective-permute-start(f32[6,16,256]{2,1,0:T(8,128)S(1)} %get-tuple-element.17), channel_id=1, source_target_pairs={{0,8},{1,9},{2,10},{3,11},{4,12},{5,13},{6,14},{7,15},{8,16},{9,17... | collective-permute-start | bytes 294920 | tf_op jit(solution)/shard_map/ppermute | solution.py:219
  10.7 17.5 %collective-permute-start.1 = (f32[6,16,256]{2,1,0:T(8,128)S(1)}, f32[6,16,256]{2,1,0:T(8,128)S(1)}, u32[]{:S(2)}, u32[]{:S(2)}) collective-permute-start(f32[6,16,256]{2,1,0:T(8,128)S(1)} %get-tuple-element.14.sent_hbm), channel_id=1, source_target_pairs={{8,0},{9,1},{10,2},{11,3},{12,4},{13,5},{14,6},{15,7},{16,8},{17,9... | collective-permute-start | bytes 294920 | tf_op jit(solution)/shard_map/ppermute | solution.py:220
  28.3 2.7 %collective-permute-start.2 = (f32[96,128]{1,0:T(8,128)S(1)}, f32[96,128]{1,0:T(8,128)S(1)}, u32[]{:S(2)}, u32[]{:S(2)}) collective-permute-start(f32[96,128]{1,0:T(8,128)S(1)} %get-tuple-element.20), channel_id=1, source_target_pairs={{0,1},{1,2},{2,3},{3,4},{4,5},{5,6},{6,7},{8,9},{9,10},{10,11},{11... | collective-permute-start | bytes 147464 | tf_op jit(solution)/shard_map/ppermute | solution.py:237
  29.7 3.1 %collective-permute-start.3 = (f32[96,128]{1,0:T(8,128)S(1)}, f32[96,128]{1,0:T(8,128)S(1)}, u32[]{:S(2)}, u32[]{:S(2)}) collective-permute-start(f32[96,128]{1,0:T(8,128)S(1)} %get-tuple-element.21), channel_id=1, source_target_pairs={{1,0},{2,1},{3,2},{4,3},{5,4},{6,5},{7,6},{9,8},{10,9},{11,10},{12... | collective-permute-start | bytes 147464 | tf_op jit(solution)/shard_map/ppermute | solution.py:238
  48.0 17.6 %collective-permute-start.4 = (f32[32,256]{1,0:T(8,128)S(1)}, f32[32,256]{1,0:T(8,128)S(1)}, u32[]{:S(2)}, u32[]{:S(2)}) collective-permute-start(f32[32,256]{1,0:T(8,128)S(1)} %reduce_sum.9), channel_id=1, source_target_pairs={{0,256},{64,320},{128,384},{192,448},{256,0},{320,64},{384,128},{4... | collective-permute-start | bytes 98312 | tf_op jit(solution)/shard_map/ppermute | solution.py:252

commit v3 on v2

--- a/solution.py
+++ b/solution.py
@@ -20,6 +20,11 @@
 F32 = jnp.float32
 
 
+def at_edges():
+    tile_id, tiles = lax.axis_index("tile"), lax.axis_size("tile")
+    return tile_id >= tiles - COL_TILES, tile_id % COL_TILES == COL_TILES - 1
+
+
 def fetch(pairs, sems):
     copies = [pltpu.make_async_copy(src, dst, sems.at[i]) for i, (src, dst) in enumerate(pairs)]
     for copy in copies:
@@ -28,7 +33,7 @@
         copy.wait()
 
 
-def row_messages(edge_ref, vec_hbm, ens_hbm, dif_hbm, weight_hbm, first_ref, last_ref, vec, ens, dif, weight, sems):
+def row_messages(vec_hbm, ens_hbm, dif_hbm, weight_hbm, first_ref, last_ref, vec, ens, dif, weight, sems):
     nrows = vec_hbm.shape[2]
     pairs = []
     for side, begin in enumerate((0, nrows - HALO)):
@@ -40,6 +45,7 @@
             (weight_hbm.at[0, rows, :], weight.at[side]),
         ]
     fetch(pairs, sems)
+    bottom, rightmost = at_edges()
     row = lax.broadcasted_iota(jnp.int32, (HALO, 256), 0)
     col = lax.broadcasted_iota(jnp.int32, (HALO, 256), 1)
     for side, ref in enumerate((first_ref, last_ref)):
@@ -48,9 +54,9 @@
                 ref[2 * m + c] = weight[side] * ens[side, m, c].astype(F32) * vec[side, c]
         row_coef, col_coef = dif[side, 0], dif[side, 1]
         if side == 1:
-            row_coef = jnp.where((row == HALO - 1) & (edge_ref[0] == 1), F32(0.0), row_coef)
+            row_coef = jnp.where((row == HALO - 1) & (bottom), F32(0.0), row_coef)
         ref[4] = row_coef
-        ref[5] = jnp.where((col == 255) & (edge_ref[1] == 1), F32(0.0), col_coef)
+        ref[5] = jnp.where((col == 255) & (rightmost), F32(0.0), col_coef)
 
 
 def pack_cols(fields):
@@ -65,7 +71,7 @@
 
 
 def own_arrays(
-    edge_ref, vec_hbm, ens_hbm, dif_hbm, weight_hbm, var_hbm, sent_hbm,
+    vec_hbm, ens_hbm, dif_hbm, weight_hbm, var_hbm, sent_hbm,
     own_ref, scale_ref, fixed_ref, first_ref, last_ref, vec, ens, dif, weight, var, sems,
 ):
     fetch(
@@ -76,6 +82,7 @@
         sems,
     )
     nrows, ncols = weight.shape
+    bottom, rightmost = at_edges()
     for m in range(2):
         for c in range(2):
             scale = weight[...] * ens[m, c].astype(F32)
@@ -83,8 +90,8 @@
             own_ref[2 * m + c] = scale * vec[c]
     row = lax.broadcasted_iota(jnp.int32, (nrows, ncols), 0)
     col = lax.broadcasted_iota(jnp.int32, (nrows, ncols), 1)
-    own_ref[4] = jnp.where((row == nrows - 1) & (edge_ref[0] == 1), F32(0.0), dif[0])
-    own_ref[5] = jnp.where((col == ncols - 1) & (edge_ref[1] == 1), F32(0.0), dif[1])
+    own_ref[4] = jnp.where((row == nrows - 1) & (bottom), F32(0.0), dif[0])
+    own_ref[5] = jnp.where((col == ncols - 1) & (rightmost), F32(0.0), dif[1])
     for c in range(2):
         fixed_ref[c] = F32(static_weight) * var[c] * vec[c]
     first_ref[...], last_ref[...] = pack_cols([own_ref[k] for k in range(6)])
@@ -186,13 +193,7 @@
 
 def local(vector, ensemble, diffusivity, norm_weight, static_var):
     tiles = lax.axis_size("tile")
-    row_tiles = tiles // COL_TILES
-    tile_id = lax.axis_index("tile")
-    edge = jnp.stack(
-        [tile_id // COL_TILES == row_tiles - 1, tile_id % COL_TILES == COL_TILES - 1]
-    ).astype(jnp.int32)
     vmem = pl.BlockSpec(memory_space=pltpu.VMEM)
-    smem = pl.BlockSpec(memory_space=pltpu.SMEM)
     hbm = pl.BlockSpec(memory_space=pltpu.HBM)
     params = pltpu.CompilerParams(vmem_limit_bytes=32 * 2**20)
 
@@ -210,10 +211,10 @@
         for x in (vector, ensemble, diffusivity, norm_weight, static_var)
     ]
     first, last = pl.pallas_call(
-        row_messages, out_shape=(f32(6, HALO, 256),) * 2, in_specs=[smem] + [hbm] * 4, out_specs=(vmem,) * 2,
+        row_messages, out_shape=(f32(6, HALO, 256),) * 2, in_specs=[hbm] * 4, out_specs=(vmem,) * 2,
         scratch_shapes=buffers(2, rows=HALO) + [pltpu.SemaphoreType.DMA((8,))],
         compiler_params=params,
-    )(edge, *held[:4])
+    )(*held[:4])
     down = [(i, i + COL_TILES) for i in range(tiles - COL_TILES)]
     up = [(b, a) for a, b in down]
     above = lax.ppermute(last, "tile", down)
@@ -222,11 +223,11 @@
     own, scale, fixed, first_own, last_own = pl.pallas_call(
         own_arrays,
         out_shape=(f32(6, 64, 256), f32(4, 64, 256), f32(2, 64, 256), f32(64, LANES), f32(64, LANES)),
-        in_specs=[smem] + [hbm] * 6, out_specs=(vmem,) * 5,
+        in_specs=[hbm] * 6, out_specs=(vmem,) * 5,
         scratch_shapes=buffers(rows=64) + [pltpu.VMEM((2, 64, 256), F32), pltpu.SemaphoreType.DMA((5,))],
         compiler_params=params,
         cost_estimate=pl.CostEstimate(flops=2 * 10**6, bytes_accessed=2 * 10**6, transcendentals=0),
-    )(edge, *held, first)
+    )(*held, first)
 
     first, last = pl.pallas_call(
         col_messages, out_shape=(f32(TALL, LANES),) * 2, in_specs=[vmem] * 4, out_specs=(vmem,) * 2,
@@ -249,8 +250,8 @@
     along_x = [[0, 1, 2, 3], [4, 5, 6, 7]]
     parts = lax.all_to_all(partial, "mem", 0, 0, axis_index_groups=along_x, tiled=True)
     mine = jnp.sum(parts, 0)
-    other = lax.ppermute(mine, "mem", [(i, (i + 4) % 8) for i in range(8)])
-    both = jnp.broadcast_to((mine + other)[None], (4, 32, 256))
+    pair = lax.all_gather(mine, "mem", axis_index_groups=[[0, 4], [1, 5], [2, 6], [3, 7]])
+    both = jnp.broadcast_to((pair[0] + pair[1])[None], (4, 32, 256))
     summed = lax.all_to_all(both, "mem", 0, 0, axis_index_groups=along_x, tiled=True)
     members = lax.axis_size("mem") * ensemble.shape[0]
     ens_part = summed.reshape(2, 64, 256) / F32(members - 1)

time: 75 us -> 73.2 us (0.976)
  blocking collectives: 18.4 us -> 34.8 us
  starting transfers between devices: 28.9 us -> 13.7 us
  waiting for transfers between devices: 17.9 us -> 16 us
  Pallas kernels: 8.5 us -> 7.42 us
    all_gather x0 -> x1, blocking collectives: none -> 16.4 us  [local(): lax.all_gather(mine, 'mem', axis_index_groups=[[0, 4], [1, 5], [2, 6], [3...]
    ppermute x1 -> x0, starting transfers between devices: 15.2 us -> none  [local(): other = lax.ppermute(mine, 'mem', [(i, (i + 4) % 8) for i in range(8)])]
    ppermute x1 -> x0, waiting for transfers between devices: 2.39 us -> none  [local(): other = lax.ppermute(mine, 'mem', [(i, (i + 4) % 8) for i in range(8)])]
  transfers between devices with their start and end apart: 5 -> 4, of which waited for: 4 -> 3; matrix products, arithmetic and copies ran while one was open for 0% -> 0% of each run, Pallas kernels for 3% -> 2%
where the time goes in v3:
time: 73.2 us; the launch traced here: 72.8 us
  blocking collectives  34.8 us (48%)
  waiting for transfers between devices  16 us (22%)
  starting transfers between devices  13.7 us (19%)
  Pallas kernels  7.42 us (10%)
    all_gather x1, blocking collectives, local(): lax.all_gather(mine, 'mem', axis_index_groups=[[0, 4], [1, 5], [2, 6], [3...  16.4 us
    ppermute x1, waiting for transfers between devices, local(): above = lax.ppermute(last, 'tile', down)  12.6 us
    all_to_all x1, blocking collectives, local(): lax.all_to_all(partial, 'mem', 0, 0, axis_index_groups=along_x, tiled=True)  10.1 us
    ppermute x1, starting transfers between devices, local(): above = lax.ppermute(last, 'tile', down)  9.1 us
    all_to_all x1, blocking collectives, local(): lax.all_to_all(both, 'mem', 0, 0, axis_index_groups=along_x, tiled=True)  8.36 us
    pallas_call x1, Pallas kernels, local(): pl.pallas_call(localize, out_shape=f32(4, 32, 256), in_specs=[vmem] * 6,...  5 us
    ppermute x1, starting transfers between devices, local(): below = lax.ppermute(first, 'tile', up)  1.92 us
    ppermute x1, waiting for transfers between devices, local(): right = lax.ppermute(first, 'tile', leftward)  1.81 us
  transfers between devices with their start and end apart: 4, of which 3 were waited for; matrix products, arithmetic and copies ran while one was open for 0% of the time, Pallas kernels for 2%

profile of v3, /device:TPU:8, one launch (start us, length us, event | category | flops | bytes accessed | tf_op | source)
XLA Modules:
  0.0 72.8 jit_solution(714427044667839047)
XLA Ops:
  0.0 0.9 %shard_map.55 = (f32[6,16,256]{2,1,0:T(8,128)S(1)}, f32[6,16,256]{2,1,0:T(8,128)S(1)}) custom-call(f32[2,1,64,256]{3,2,1,0:T(8,128)} %vec_hbm.3, bf16[2,2,1,64,256]{4,3,2,1,0:T(8,128)(2,1)} %ens_hbm.3, f32[2,1,64,256]{3,2,1,0:T(8,128)} %dif_hbm.3, f32[1,64,256]{2,1,0:T(8,128)} %weight_hbm.3), custom_call_target="tpu_custom_call" | custom-call | tf_op jit(solution)/shard_map/pallas_call | solution.py:213
  1.0 9.1 %collective-permute-start = (f32[6,16,256]{2,1,0:T(8,128)S(1)}, f32[6,16,256]{2,1,0:T(8,128)S(1)}, u32[]{:S(2)}, u32[]{:S(2)}) collective-permute-start(f32[6,16,256]{2,1,0:T(8,128)S(1)} %get-tuple-element.17), channel_id=1, source_target_pairs={{0,8},{1,9},{2,10},{3,11},{4,12},{5,13},{6,14},{7,15},{8,16},{9,17... | collective-permute-start | bytes 294920 | tf_op jit(solution)/shard_map/ppermute | solution.py:220
  10.1 1.9 %collective-permute-start.1 = (f32[6,16,256]{2,1,0:T(8,128)S(1)}, f32[6,16,256]{2,1,0:T(8,128)S(1)}, u32[]{:S(2)}, u32[]{:S(2)}) collective-permute-start(f32[6,16,256]{2,1,0:T(8,128)S(1)} %get-tuple-element.14.sent_hbm), channel_id=1, source_target_pairs={{8,0},{9,1},{10,2},{11,3},{12,4},{13,5},{14,6},{15,7},{16,8},{17,9... | collective-permute-start | bytes 294920 | tf_op jit(solution)/shard_map/ppermute | solution.py:221
  12.0 1.4 %shard_map.56 = (f32[6,64,256]{2,1,0:T(8,128)S(1)}, f32[4,64,256]{2,1,0:T(8,128)S(1)}, f32[2,64,256]{2,1,0:T(8,128)S(1)}, f32[64,128]{1,0:T(8,128)S(1)}, f32[64,128]{1,0:T(8,128)S(1)}) custom-call(f32[2,1,64,256]{3,2,1,0:T(8,128)} %vec_hbm.3, bf16[2,2,1,64,256]{4,3,2,1,0:T(8,128)(2,1)} %ens_hbm.3, f32[2,1,64,256]{3,2,1,0:T(8,128)} %dif_hbm.3, ...), custom_call_target="tpu_custom_call" | custom-call | flops 2000000 | bytes 2000000 | tf_op jit(solution)/shard_map/pallas_call | solution.py:223
  13.4 12.6 %collective-permute-done.above_ref = f32[6,16,256]{2,1,0:T(8,128)S(1)} collective-permute-done((f32[6,16,256]{2,1,0:T(8,128)S(1)}, f32[6,16,256]{2,1,0:T(8,128)S(1)}, u32[]{:S(2)}, u32[]{:S(2)}) %collective-permute-start) | collective-permute-done | bytes 98336 | tf_op jit(solution)/shard_map/ppermute | solution.py:220
  25.9 1.6 %collective-permute-done.1.below_ref = f32[6,16,256]{2,1,0:T(8,128)S(1)} collective-permute-done((f32[6,16,256]{2,1,0:T(8,128)S(1)}, f32[6,16,256]{2,1,0:T(8,128)S(1)}, u32[]{:S(2)}, u32[]{:S(2)}) %collective-permute-start.1) | collective-permute-done | bytes 98336 | tf_op jit(solution)/shard_map/ppermute | solution.py:221
  27.6 0.1 shard_map.57
  27.7 1.4 %collective-permute-start.2 = (f32[96,128]{1,0:T(8,128)S(1)}, f32[96,128]{1,0:T(8,128)S(1)}, u32[]{:S(2)}, u32[]{:S(2)}) collective-permute-start(f32[96,128]{1,0:T(8,128)S(1)} %get-tuple-element.20), channel_id=1, source_target_pairs={{0,1},{1,2},{2,3},{3,4},{4,5},{5,6},{6,7},{8,9},{9,10},{10,11},{11... | collective-permute-start | bytes 147464 | tf_op jit(solution)/shard_map/ppermute | solution.py:238
  29.1 1.3 %collective-permute-start.3 = (f32[96,128]{1,0:T(8,128)S(1)}, f32[96,128]{1,0:T(8,128)S(1)}, u32[]{:S(2)}, u32[]{:S(2)}) collective-permute-start(f32[96,128]{1,0:T(8,128)S(1)} %get-tuple-element.21), channel_id=1, source_target_pairs={{1,0},{2,1},{3,2},{4,3},{5,4},{6,5},{7,6},{9,8},{10,9},{11,10},{12... | collective-permute-start | bytes 147464 | tf_op jit(solution)/shard_map/ppermute | solution.py:239
  30.4 0.0 collective-permute-done.2.left_ref
  30.4 1.8 %collective-permute-done.3.right_ref = f32[96,128]{1,0:T(8,128)S(1)} collective-permute-done((f32[96,128]{1,0:T(8,128)S(1)}, f32[96,128]{1,0:T(8,128)S(1)}, u32[]{:S(2)}, u32[]{:S(2)}) %collective-permute-start.3) | collective-permute-done | bytes 49184 | tf_op jit(solution)/shard_map/ppermute | solution.py:239
  32.3 5.0 %shard_map.58 = f32[4,32,256]{2,1,0:T(8,128)S(1)} custom-call(f32[6,64,256]{2,1,0:T(8,128)S(1)} %get-tuple-element.15.own_ref, f32[4,64,256]{2,1,0:T(8,128)S(1)} %get-tuple-element.16.scale_ref, f32[6,16,256]{2,1,0:T(8,128)S(1)} %collective-permute-done.above_ref, f32[6,16,256]{2,1,0:T(8,128)S(1)} %collective-permute-done.1.below_ref, ...), custom_call_target="tpu_custom_call" | custom-call | tf_op jit(solution)/shard_map/pallas_call | solution.py:241
  37.3 10.1 %all_to_all.10 = f32[4,32,256]{2,1,0:T(8,128)S(1)} all-to-all(f32[4,32,256]{2,1,0:T(8,128)S(1)} %shard_map.58), channel_id=1, replica_groups={{0,64,128,192},{256,320,384,448},{1,65,129,193},{257,321,385,449},{2,66..., dimensions={0} | all-to-all | bytes 262144 | tf_op jit(solution)/shard_map/all_to_all | solution.py:251
  47.4 16.4 %all-gather = f32[64,256]{1,0:T(8,128)S(1)} all-gather(f32[32,256]{1,0:T(8,128)S(1)} %reduce_sum.9), channel_id=2, replica_groups={{0,256},{64,320},{128,384},{192,448},{1,257},{65,321},{129,385},{193,44..., dimensions={0}, use_global_device_ids=true | all-gather | bytes 98304 | tf_op jit(solution)/shard_map/all_gather | solution.py:253
  63.8 8.4 %all_to_all.11 = f32[4,32,256]{2,1,0:T(8,128)S(1)} all-to-all(f32[4,32,256]{2,1,0:T(8,128)S(1)} %broadcast_in_dim.12), channel_id=1, replica_groups={{0,64,128,192},{256,320,384,448},{1,65,129,193},{257,321,385,449},{2,66..., dimensions={0} | all-to-all | bytes 262144 | tf_op jit(solution)/shard_map/all_to_all | solution.py:255
  72.1 0.7 fusion
  (4 shorter events, 0.0 us)
Async XLA Ops:
  1.0 25.0 %collective-permute-start = (f32[6,16,256]{2,1,0:T(8,128)S(1)}, f32[6,16,256]{2,1,0:T(8,128)S(1)}, u32[]{:S(2)}, u32[]{:S(2)}) collective-permute-start(f32[6,16,256]{2,1,0:T(8,128)S(1)} %get-tuple-element.17), channel_id=1, source_target_pairs={{0,8},{1,9},{2,10},{3,11},{4,12},{5,13},{6,14},{7,15},{8,16},{9,17... | collective-permute-start | bytes 294920 | tf_op jit(solution)/shard_map/ppermute | solution.py:220
  10.1 17.5 %collective-permute-start.1 = (f32[6,16,256]{2,1,0:T(8,128)S(1)}, f32[6,16,256]{2,1,0:T(8,128)S(1)}, u32[]{:S(2)}, u32[]{:S(2)}) collective-permute-start(f32[6,16,256]{2,1,0:T(8,128)S(1)} %get-tuple-element.14.sent_hbm), channel_id=1, source_target_pairs={{8,0},{9,1},{10,2},{11,3},{12,4},{13,5},{14,6},{15,7},{16,8},{17,9... | collective-permute-start | bytes 294920 | tf_op jit(solution)/shard_map/ppermute | solution.py:221
  27.7 2.7 %collective-permute-start.2 = (f32[96,128]{1,0:T(8,128)S(1)}, f32[96,128]{1,0:T(8,128)S(1)}, u32[]{:S(2)}, u32[]{:S(2)}) collective-permute-start(f32[96,128]{1,0:T(8,128)S(1)} %get-tuple-element.20), channel_id=1, source_target_pairs={{0,1},{1,2},{2,3},{3,4},{4,5},{5,6},{6,7},{8,9},{9,10},{10,11},{11... | collective-permute-start | bytes 147464 | tf_op jit(solution)/shard_map/ppermute | solution.py:238
  29.1 3.1 %collective-permute-start.3 = (f32[96,128]{1,0:T(8,128)S(1)}, f32[96,128]{1,0:T(8,128)S(1)}, u32[]{:S(2)}, u32[]{:S(2)}) collective-permute-start(f32[96,128]{1,0:T(8,128)S(1)} %get-tuple-element.21), channel_id=1, source_target_pairs={{1,0},{2,1},{3,2},{4,3},{5,4},{6,5},{7,6},{9,8},{10,9},{11,10},{12... | collective-permute-start | bytes 147464 | tf_op jit(solution)/shard_map/ppermute | solution.py:239

commit v4 on v3

--- a/solution.py
+++ b/solution.py
@@ -97,13 +97,13 @@
     first_ref[...], last_ref[...] = pack_cols([own_ref[k] for k in range(6)])
 
 
-def col_messages(first_own, last_own, above_ref, below_ref, first_ref, last_ref):
-    for rows, ref in ((slice(0, HALO), above_ref), (slice(TALL - HALO, TALL), below_ref)):
+def corner_messages(above_ref, below_ref, sent_ref, first_ref, last_ref):
+    for side, ref in enumerate((above_ref, below_ref)):
+        rows = slice(HALO * side, HALO * side + HALO)
         first_ref[rows, :], last_ref[rows, :] = pack_cols([ref[k] for k in range(6)])
-    first_ref[HALO:-HALO, :] = first_own[...]
-    last_ref[HALO:-HALO, :] = last_own[...]
-
-
+
+
+EARLY = 4
 PAD = 8
 COLUMNS = RING // LANES
 
@@ -132,50 +132,125 @@
             dst[j, p : p + 8, :] = x + rows + cols
 
 
+def ring(fields, left, right, picks):
+    nrows = left.shape[0]
+    lane = lax.broadcasted_iota(jnp.int32, (nrows, LANES), 1)
+
+    def padded(k):
+        after = pltpu.roll(right, LANES - k * HALO, 1) if k else right
+        before = pltpu.roll(left, LANES - (k + 1) * HALO, 1)
+        edge = jnp.where(lane < HALO, after, jnp.where(lane >= LANES - HALO, before, F32(0.0)))
+        return jnp.concatenate([fields[k], edge], 1)
+
+    made = {k: padded(k) for k in set(picks)}
+    tiles, tail = [], None
+    for f, k in enumerate(picks):
+        part = pltpu.roll(made[k], 32 * f, 1) if f else made[k]
+        begin = part[:, :LANES]
+        tiles += [jnp.where(lane < 32 * f - HALO, tail, begin) if f else begin, part[:, LANES:256]]
+        tail = part[:, 256:]
+        wrap = tail if f == 0 else wrap
+    return tiles + [jnp.where(lane < LANES - HALO, tail, wrap)]
+
+
+def lay(fields, left, right, rows, a_ref, row_ref, col_ref):
+    for ref, picks in ((a_ref, (0, 1, 2, 3)), (row_ref, (4,) * 4), (col_ref, (5,) * 4)):
+        for j, tile in enumerate(ring(fields, left, right, picks)):
+            ref[j, rows, :] = tile
+
+
+def lay_west(col_ref, west_ref, rows):
+    lane = lax.broadcasted_iota(jnp.int32, (rows.stop - rows.start, LANES), 1)
+    for j in range(COLUMNS):
+        before = pltpu.roll(col_ref[(j - 1) % COLUMNS, rows, :], 1, 1)
+        west_ref[j, rows, :] = jnp.where(lane == 0, before, pltpu.roll(col_ref[j, rows, :], 1, 1))
+
+
+def group(ref, g):
+    return ref[:, PAD + 8 * g : PAD + 8 * g + 8, :]
+
+
+def keep_and_sweep(first_ref, second_ref, row_ref, col_ref, west_ref, outer, top_ref, bottom_ref, count):
+    def two(i, carry):
+        for s, (src, dst) in enumerate(((first_ref, second_ref), (second_ref, first_ref))):
+            top_ref[2 * i + s] = group(src, outer + 1)
+            bottom_ref[2 * i + s] = group(src, 6 - outer)
+            sweep(src, dst, row_ref, col_ref, west_ref, outer, 8 - outer)
+        return carry
+
+    lax.fori_loop(0, count // 2, two, 0)
+
+
+def interior_first(
+    own_ref, left_ref, right_ref, start_ref, row_ref, col_ref, west_ref, half_ref, top_ref, bottom_ref, other_ref
+):
+    own = slice(PAD, PAD + 64)
+    for ref in (row_ref, half_ref, other_ref):
+        ref[:, :PAD, :] = jnp.zeros((COLUMNS, PAD, LANES), F32)
+        ref[:, PAD + 64 :, :] = jnp.zeros((COLUMNS, PAD, LANES), F32)
+    lay([own_ref[k] for k in range(6)], left_ref[...], right_ref[...], own, start_ref, row_ref, col_ref)
+    lay_west(col_ref, west_ref, own)
+    half_ref[:, own, :] = start_ref[:, own, :]
+    keep_and_sweep(half_ref, other_ref, row_ref, col_ref, west_ref, 0, top_ref, bottom_ref, EARLY)
+
+
+def interior_second(
+    quarter_ref, row_ref, col_ref, west_ref, sent_ref,
+    top_mid, bottom_mid, half_ref, top_ref, bottom_ref, final_ref, a_ref, b_ref
+):
+    a_ref[...] = quarter_ref[...]
+    b_ref[:, :PAD, :] = quarter_ref[:, :PAD, :]
+    b_ref[:, PAD + 64 :, :] = quarter_ref[:, PAD + 64 :, :]
+    keep_and_sweep(a_ref, b_ref, row_ref, col_ref, west_ref, 0, top_mid, bottom_mid, SWEEPS - EARLY)
+    half_ref[0] = group(a_ref, 1)
+    half_ref[1] = group(a_ref, 6)
+    keep_and_sweep(a_ref, b_ref, row_ref, col_ref, west_ref, 1, top_ref, bottom_ref, SWEEPS)
+    final_ref[...] = a_ref[:, PAD + 16 : PAD + 48, :]
+
+
 def localize(
-    own_ref, scale_ref, above_ref, below_ref, left_ref, right_ref,
+    scale_ref, above_ref, below_ref, left_ref, right_ref,
+    own_ref, own_row, own_col, top_first, bottom_first, top_mid, bottom_mid, half_ref, top_second, bottom_second, final_ref,
     out_ref, a_ref, b_ref, row_ref, col_ref, west_ref,
 ):
-    lane = lax.broadcasted_iota(jnp.int32, (TALL, LANES), 1)
-    tall = slice(PAD, PAD + TALL)
-
-    def padded(k):
-        right = pltpu.roll(right_ref[...], (LANES - k * HALO) % LANES, 1) if k else right_ref[...]
-        left = pltpu.roll(left_ref[...], LANES - (k + 1) * HALO, 1)
-        edge = jnp.where(lane < HALO, right, jnp.where(lane >= LANES - HALO, left, F32(0.0)))
-        return jnp.concatenate([jnp.concatenate([above_ref[k], own_ref[k], below_ref[k]], 0), edge], 1)
-
-    def lay(ref, parts):
-        for f in range(FIELDS):
-            part = pltpu.roll(parts[f], 32 * f, 1) if f else parts[f]
-            if f:
-                ref[2 * f, tall, :] = jnp.where(lane < 32 * f - HALO, tail, part[:, :LANES])
-            else:
-                ref[0, tall, :] = part[:, :LANES]
-                wrap = part[:, 256:]
-            ref[2 * f + 1, tall, :] = part[:, LANES:256]
-            tail = part[:, 256:]
-        ref[COLUMNS - 1, tall, :] = jnp.where(lane < LANES - HALO, tail, wrap)
-
     for ref in (a_ref, b_ref, row_ref):
         ref[:, :PAD, :] = jnp.zeros((COLUMNS, PAD, LANES), F32)
         ref[:, PAD + TALL :, :] = jnp.zeros((COLUMNS, PAD, LANES), F32)
-    lay(a_ref, [padded(f) for f in range(FIELDS)])
-    lay(row_ref, [padded(4)] * FIELDS)
-    lay(col_ref, [padded(5)] * FIELDS)
-    for j in range(COLUMNS):
-        before = pltpu.roll(col_ref[(j - 1) % COLUMNS, tall, :], 1, 1)
-        west_ref[j, tall, :] = jnp.where(lane == 0, before, pltpu.roll(col_ref[j, tall, :], 1, 1))
-
-    def two(begin, end):
-        def body(_, carry):
-            sweep(a_ref, b_ref, row_ref, col_ref, west_ref, begin, end)
-            sweep(b_ref, a_ref, row_ref, col_ref, west_ref, begin, end)
+    for side, (ref, begin) in enumerate(((above_ref, 0), (below_ref, TALL - HALO))):
+        rows = slice(HALO * side, HALO * side + HALO)
+        there = slice(PAD + begin, PAD + begin + HALO)
+        fields = [ref[k] for k in range(6)]
+        lay(fields, left_ref[rows, :], right_ref[rows, :], there, a_ref, row_ref, col_ref)
+    for begin, end in ((0, 16), (40, 64)):
+        here, there = slice(PAD + begin, PAD + end), slice(PAD + HALO + begin, PAD + HALO + end)
+        row_ref[:, there, :] = own_row[:, here, :]
+        col_ref[:, there, :] = own_col[:, here, :]
+        a_ref[:, there, :] = own_ref[:, here, :]
+    lay_west(col_ref, west_ref, slice(PAD, PAD + 32))
+    lay_west(col_ref, west_ref, slice(PAD + 56, PAD + TALL))
+
+    def put(ref, g, block):
+        ref[:, PAD + 8 * g : PAD + 8 * g + 8, :] = block
+
+    def several(outer, top_ref, bottom_ref, count):
+        def two(i, carry):
+            for s, (src, dst) in enumerate(((a_ref, b_ref), (b_ref, a_ref))):
+                put(src, 3 + outer, top_ref[2 * i + s])
+                put(src, 8 - outer, bottom_ref[2 * i + s])
+                sweep(src, dst, row_ref, col_ref, west_ref, outer, 3 + outer)
+                sweep(src, dst, row_ref, col_ref, west_ref, 9 - outer, GROUPS - outer)
             return carry
-        return body
-
-    lax.fori_loop(0, SWEEPS // 2, two(0, GROUPS), 0)
-    lax.fori_loop(0, SWEEPS // 2, two(1, GROUPS - 1), 0)
+
+        lax.fori_loop(0, count // 2, two, 0)
+
+    b_ref[:, PAD : PAD + 40, :] = a_ref[:, PAD : PAD + 40, :]
+    b_ref[:, PAD + 56 : PAD + TALL, :] = a_ref[:, PAD + 56 : PAD + TALL, :]
+    several(0, top_first, bottom_first, EARLY)
+    several(0, top_mid, bottom_mid, SWEEPS - EARLY)
+    put(a_ref, 3, half_ref[0])
+    put(a_ref, 8, half_ref[1])
+    several(1, top_second, bottom_second, SWEEPS)
+    a_ref[:, PAD + 32 : PAD + 64, :] = final_ref[...]
 
     inner = slice(PAD + HALO, PAD + TALL - HALO)
     for c in range(2):
@@ -229,23 +304,49 @@
         cost_estimate=pl.CostEstimate(flops=2 * 10**6, bytes_accessed=2 * 10**6, transcendentals=0),
     )(*held, first)
 
-    first, last = pl.pallas_call(
-        col_messages, out_shape=(f32(TALL, LANES),) * 2, in_specs=[vmem] * 4, out_specs=(vmem,) * 2,
-        compiler_params=params,
-    )(first_own, last_own, above, below)
     rightward = [(i, i + 1) for i in range(tiles) if (i + 1) % COL_TILES]
     leftward = [(b, a) for a, b in rightward]
+    left = lax.ppermute(last_own, "tile", rightward)
+    right = lax.ppermute(first_own, "tile", leftward)
+
+    rings = (COLUMNS, 64 + 2 * PAD, LANES)
+    def edges(count):
+        return (f32(count, COLUMNS, 8, LANES),) * 2
+
+    start, row_ring, col_ring, west_ring, quarter, *first_edges = pl.pallas_call(
+        interior_first,
+        out_shape=(f32(*rings),) * 5 + edges(EARLY),
+        in_specs=[vmem] * 3, out_specs=(vmem,) * 7,
+        scratch_shapes=[pltpu.VMEM(rings, F32)],
+        compiler_params=params,
+        cost_estimate=pl.CostEstimate(flops=5 * 10**6, bytes_accessed=4 * 10**6, transcendentals=0),
+    )(own, left, right)
+
+    first, last = pl.pallas_call(
+        corner_messages, out_shape=(f32(2 * HALO, LANES),) * 2, in_specs=[vmem] * 3, out_specs=(vmem,) * 2,
+        compiler_params=params,
+    )(above, below, quarter)
     left = lax.ppermute(last, "tile", rightward)
     right = lax.ppermute(first, "tile", leftward)
+    second = pl.pallas_call(
+        interior_second,
+        out_shape=edges(SWEEPS - EARLY) + (f32(2, COLUMNS, 8, LANES),) + edges(SWEEPS) + (f32(COLUMNS, 32, LANES),),
+        in_specs=[vmem] * 5, out_specs=(vmem,) * 6,
+        scratch_shapes=[pltpu.VMEM(rings, F32)] * 2,
+        compiler_params=params,
+        cost_estimate=pl.CostEstimate(flops=5 * 10**6, bytes_accessed=4 * 10**6, transcendentals=0),
+    )(quarter, row_ring, col_ring, west_ring, first)
 
     partial = pl.pallas_call(
         localize,
         out_shape=f32(4, 32, 256),
-        in_specs=[vmem] * 6,
+        in_specs=[vmem] * 16,
         out_specs=vmem,
         scratch_shapes=[pltpu.VMEM((COLUMNS, TALL + 2 * PAD, LANES), F32)] * 5,
         compiler_params=params,
-    )(own, scale, above, below, left, right)
+    )(
+        scale, above, below, left, right, start, row_ring, col_ring, *first_edges, *second
+    )
 
     along_x = [[0, 1, 2, 3], [4, 5, 6, 7]]
     parts = lax.all_to_all(partial, "mem", 0, 0, axis_index_groups=along_x, tiled=True)

time: 73.2 us -> 72.5 us (level)
  the two profiles are of different devices: /device:TPU:8 before, /device:TPU:80 now
where the time goes in v4:
time: 72.5 us; the launch traced here: 72.1 us
  blocking collectives  36.8 us (51%)
  starting transfers between devices  21.6 us (30%)
  Pallas kernels  9.5 us (13%)
  waiting for transfers between devices  3.37 us (5%)
    all_gather x1, blocking collectives, local(): lax.all_gather(mine, 'mem', axis_index_groups=[[0, 4], [1, 5], [2, 6], [3...  18.4 us
    all_to_all x1, blocking collectives, local(): lax.all_to_all(partial, 'mem', 0, 0, axis_index_groups=along_x, tiled=True)  10.1 us
    ppermute x1, starting transfers between devices, local(): below = lax.ppermute(first, 'tile', up)  8.98 us
    all_to_all x1, blocking collectives, local(): lax.all_to_all(both, 'mem', 0, 0, axis_index_groups=along_x, tiled=True)  8.36 us
    ppermute x1, starting transfers between devices, local(): right = lax.ppermute(first_own, 'tile', leftward)  3.64 us
    pallas_call x1, Pallas kernels, local(): pl.pallas_call(localize, out_shape=f32(4, 32, 256), in_specs=[vmem] * 16,...  3.29 us
    ppermute x1, starting transfers between devices, local(): right = lax.ppermute(first, 'tile', leftward)  2.79 us
    ppermute x1, starting transfers between devices, local(): left = lax.ppermute(last, 'tile', rightward)  2.21 us
  transfers between devices with their start and end apart: 6, of which 3 were waited for; matrix products, arithmetic and copies ran while one was open for 0% of the time, Pallas kernels for 7%

profile of v4, /device:TPU:80, one launch (start us, length us, event | category | flops | bytes accessed | tf_op | source)
XLA Modules:
  0.0 72.1 jit_solution(1903505439255283232)
XLA Ops:
  0.0 0.9 %shard_map.55 = (f32[6,16,256]{2,1,0:T(8,128)S(1)}, f32[6,16,256]{2,1,0:T(8,128)S(1)}) custom-call(f32[2,1,64,256]{3,2,1,0:T(8,128)} %vec_hbm.3, bf16[2,2,1,64,256]{4,3,2,1,0:T(8,128)(2,1)} %ens_hbm.3, f32[2,1,64,256]{3,2,1,0:T(8,128)} %dif_hbm.3, f32[1,64,256]{2,1,0:T(8,128)} %weight_hbm.3), custom_call_target="tpu_custom_call" | custom-call | tf_op jit(solution)/shard_map/pallas_call | solution.py:288
  1.0 9.0 %collective-permute-start.1 = (f32[6,16,256]{2,1,0:T(8,128)S(1)}, f32[6,16,256]{2,1,0:T(8,128)S(1)}, u32[]{:S(2)}, u32[]{:S(2)}) collective-permute-start(f32[6,16,256]{2,1,0:T(8,128)S(1)} %get-tuple-element.27.sent_hbm), channel_id=1, source_target_pairs={{8,0},{9,1},{10,2},{11,3},{12,4},{13,5},{14,6},{15,7},{16,8},{17,9... | collective-permute-start | bytes 294920 | tf_op jit(solution)/shard_map/ppermute | solution.py:296
  9.9 2.0 %collective-permute-start = (f32[6,16,256]{2,1,0:T(8,128)S(1)}, f32[6,16,256]{2,1,0:T(8,128)S(1)}, u32[]{:S(2)}, u32[]{:S(2)}) collective-permute-start(f32[6,16,256]{2,1,0:T(8,128)S(1)} %get-tuple-element.29), channel_id=1, source_target_pairs={{0,8},{1,9},{2,10},{3,11},{4,12},{5,13},{6,14},{7,15},{8,16},{9,17... | collective-permute-start | bytes 294920 | tf_op jit(solution)/shard_map/ppermute | solution.py:295
  12.0 1.4 %shard_map.56 = (f32[6,64,256]{2,1,0:T(8,128)S(1)}, f32[4,64,256]{2,1,0:T(8,128)S(1)}, f32[2,64,256]{2,1,0:T(8,128)S(1)}, f32[64,128]{1,0:T(8,128)S(1)}, f32[64,128]{1,0:T(8,128)S(1)}) custom-call(f32[2,1,64,256]{3,2,1,0:T(8,128)} %vec_hbm.3, bf16[2,2,1,64,256]{4,3,2,1,0:T(8,128)(2,1)} %ens_hbm.3, f32[2,1,64,256]{3,2,1,0:T(8,128)} %dif_hbm.3, ...), custom_call_target="tpu_custom_call" | custom-call | flops 2000000 | bytes 2000000 | tf_op jit(solution)/shard_map/pallas_call | solution.py:298
  13.4 1.9 %collective-permute-start.2 = (f32[64,128]{1,0:T(8,128)S(1)}, f32[64,128]{1,0:T(8,128)S(1)}, u32[]{:S(2)}, u32[]{:S(2)}) collective-permute-start(f32[64,128]{1,0:T(8,128)S(1)} %get-tuple-element.31), channel_id=1, source_target_pairs={{0,1},{1,2},{2,3},{3,4},{4,5},{5,6},{6,7},{8,9},{9,10},{10,11},{11... | collective-permute-start | bytes 98312 | tf_op jit(solution)/shard_map/ppermute | solution.py:309
  15.3 3.6 %collective-permute-start.3 = (f32[64,128]{1,0:T(8,128)S(1)}, f32[64,128]{1,0:T(8,128)S(1)}, u32[]{:S(2)}, u32[]{:S(2)}) collective-permute-start(f32[64,128]{1,0:T(8,128)S(1)} %get-tuple-element.32), channel_id=1, source_target_pairs={{1,0},{2,1},{3,2},{4,3},{5,4},{6,5},{7,6},{9,8},{10,9},{11,10},{12... | collective-permute-start | bytes 98312 | tf_op jit(solution)/shard_map/ppermute | solution.py:310
  18.9 0.0 collective-permute-done.2.left_ref
  19.0 1.6 %collective-permute-done.3.right_ref = f32[64,128]{1,0:T(8,128)S(1)} collective-permute-done((f32[64,128]{1,0:T(8,128)S(1)}, f32[64,128]{1,0:T(8,128)S(1)}, u32[]{:S(2)}, u32[]{:S(2)}) %collective-permute-start.3) | collective-permute-done | bytes 32800 | tf_op jit(solution)/shard_map/ppermute | solution.py:310
  20.5 1.6 %shard_map.57 = (f32[9,80,128]{2,1,0:T(8,128)S(1)}, f32[9,80,128]{2,1,0:T(8,128)S(1)}, f32[9,80,128]{2,1,0:T(8,128)S(1)}, f32[9,80,128]{2,1,0:T(8,128)S(1)}, f32...) custom-call(f32[6,64,256]{2,1,0:T(8,128)S(1)} %get-tuple-element.30.own_ref, ...), custom_call_target="tpu_custom_call" | custom-call | flops 5000000 | bytes 4000000 | tf_op jit(solution)/shard_map/pallas_call | solution.py:316
  22.1 0.0 collective-permute-done.1.below_ref
  22.1 1.2 %collective-permute-done.above_ref = f32[6,16,256]{2,1,0:T(8,128)S(1)} collective-permute-done((f32[6,16,256]{2,1,0:T(8,128)S(1)}, f32[6,16,256]{2,1,0:T(8,128)S(1)}, u32[]{:S(2)}, u32[]{:S(2)}) %collective-permute-start) | collective-permute-done | bytes 98336 | tf_op jit(solution)/shard_map/ppermute | solution.py:295
  23.3 0.1 shard_map.58
  23.4 2.8 %collective-permute-start.5 = (f32[32,128]{1,0:T(8,128)S(1)}, f32[32,128]{1,0:T(8,128)S(1)}, u32[]{:S(2)}, u32[]{:S(2)}) collective-permute-start(f32[32,128]{1,0:T(8,128)S(1)} %get-tuple-element.35.sent_ref), channel_id=1, source_target_pairs={{1,0},{2,1},{3,2},{4,3},{5,4},{6,5},{7,6},{9,8},{10,9},{11,10},{12... | collective-permute-start | bytes 49160 | tf_op jit(solution)/shard_map/ppermute | solution.py:330
  26.2 2.2 %collective-permute-start.4 = (f32[32,128]{1,0:T(8,128)S(1)}, f32[32,128]{1,0:T(8,128)S(1)}, u32[]{:S(2)}, u32[]{:S(2)}) collective-permute-start(f32[32,128]{1,0:T(8,128)S(1)} %get-tuple-element.34), channel_id=1, source_target_pairs={{0,1},{1,2},{2,3},{3,4},{4,5},{5,6},{6,7},{8,9},{9,10},{10,11},{11... | collective-permute-start | bytes 49160 | tf_op jit(solution)/shard_map/ppermute | solution.py:329
  28.4 2.2 %shard_map.59 = (f32[4,9,8,128]{3,2,1,0:T(8,128)S(1)}, f32[4,9,8,128]{3,2,1,0:T(8,128)S(1)}, f32[2,9,8,128]{3,2,1,0:T(8,128)S(1)}, f32[8,9,8,128]{3,2,1,0:T(8,12...) custom-call(f32[9,80,128]{2,1,0:T(8,128)S(1)} %get-tuple-element.33.sent_ref.quarter_ref, ...), custom_call_target="tpu_custom_call" | custom-call | flops 5000000 | bytes 4000000 | tf_op jit(solution)/shard_map/pallas_call | solution.py:331
  30.6 0.0 collective-permute-done.5.right_ref
  30.6 0.6 collective-permute-done.4.left_ref
  31.3 3.3 %shard_map.60 = f32[4,32,256]{2,1,0:T(8,128)S(1)} custom-call(f32[4,64,256]{2,1,0:T(8,128)S(1)} %get-tuple-element.28.scale_ref, f32[6,16,256]{2,1,0:T(8,128)S(1)} %collective-permute-done.above_ref, f32[6,16,256]{2,1,0:T(8,128)S(1)} %collective-permute-done.1.below_ref, f32[32,128]{1,0:T(8,128)S(1)} %collective-permute-done.4.left_ref, ...), custom_call_target="tpu_custom_call" | custom-call | tf_op jit(solution)/shard_map/pallas_call | solution.py:340
  34.6 10.1 %all_to_all.10 = f32[4,32,256]{2,1,0:T(8,128)S(1)} all-to-all(f32[4,32,256]{2,1,0:T(8,128)S(1)} %shard_map.60), channel_id=1, replica_groups={{0,64,128,192},{256,320,384,448},{1,65,129,193},{257,321,385,449},{2,66..., dimensions={0} | all-to-all | bytes 262144 | tf_op jit(solution)/shard_map/all_to_all | solution.py:352
  44.7 18.4 %all-gather = f32[64,256]{1,0:T(8,128)S(1)} all-gather(f32[32,256]{1,0:T(8,128)S(1)} %reduce_sum.9), channel_id=2, replica_groups={{0,256},{64,320},{128,384},{192,448},{1,257},{65,321},{129,385},{193,44..., dimensions={0}, use_global_device_ids=true | all-gather | bytes 98304 | tf_op jit(solution)/shard_map/all_gather | solution.py:354
  63.0 8.4 %all_to_all.11 = f32[4,32,256]{2,1,0:T(8,128)S(1)} all-to-all(f32[4,32,256]{2,1,0:T(8,128)S(1)} %broadcast_in_dim.12), channel_id=1, replica_groups={{0,64,128,192},{256,320,384,448},{1,65,129,193},{257,321,385,449},{2,66..., dimensions={0} | all-to-all | bytes 262144 | tf_op jit(solution)/shard_map/all_to_all | solution.py:356
  71.4 0.7 fusion
  (4 shorter events, 0.0 us)
Async XLA Ops:
  1.0 21.2 %collective-permute-start.1 = (f32[6,16,256]{2,1,0:T(8,128)S(1)}, f32[6,16,256]{2,1,0:T(8,128)S(1)}, u32[]{:S(2)}, u32[]{:S(2)}) collective-permute-start(f32[6,16,256]{2,1,0:T(8,128)S(1)} %get-tuple-element.27.sent_hbm), channel_id=1, source_target_pairs={{8,0},{9,1},{10,2},{11,3},{12,4},{13,5},{14,6},{15,7},{16,8},{17,9... | collective-permute-start | bytes 294920 | tf_op jit(solution)/shard_map/ppermute | solution.py:296
  9.9 13.4 %collective-permute-start = (f32[6,16,256]{2,1,0:T(8,128)S(1)}, f32[6,16,256]{2,1,0:T(8,128)S(1)}, u32[]{:S(2)}, u32[]{:S(2)}) collective-permute-start(f32[6,16,256]{2,1,0:T(8,128)S(1)} %get-tuple-element.29), channel_id=1, source_target_pairs={{0,8},{1,9},{2,10},{3,11},{4,12},{5,13},{6,14},{7,15},{8,16},{9,17... | collective-permute-start | bytes 294920 | tf_op jit(solution)/shard_map/ppermute | solution.py:295
  13.4 5.6 %collective-permute-start.2 = (f32[64,128]{1,0:T(8,128)S(1)}, f32[64,128]{1,0:T(8,128)S(1)}, u32[]{:S(2)}, u32[]{:S(2)}) collective-permute-start(f32[64,128]{1,0:T(8,128)S(1)} %get-tuple-element.31), channel_id=1, source_target_pairs={{0,1},{1,2},{2,3},{3,4},{4,5},{5,6},{6,7},{8,9},{9,10},{10,11},{11... | collective-permute-start | bytes 98312 | tf_op jit(solution)/shard_map/ppermute | solution.py:309
  15.3 5.2 %collective-permute-start.3 = (f32[64,128]{1,0:T(8,128)S(1)}, f32[64,128]{1,0:T(8,128)S(1)}, u32[]{:S(2)}, u32[]{:S(2)}) collective-permute-start(f32[64,128]{1,0:T(8,128)S(1)} %get-tuple-element.32), channel_id=1, source_target_pairs={{1,0},{2,1},{3,2},{4,3},{5,4},{6,5},{7,6},{9,8},{10,9},{11,10},{12... | collective-permute-start | bytes 98312 | tf_op jit(solution)/shard_map/ppermute | solution.py:310
  23.4 7.2 %collective-permute-start.5 = (f32[32,128]{1,0:T(8,128)S(1)}, f32[32,128]{1,0:T(8,128)S(1)}, u32[]{:S(2)}, u32[]{:S(2)}) collective-permute-start(f32[32,128]{1,0:T(8,128)S(1)} %get-tuple-element.35.sent_ref), channel_id=1, source_target_pairs={{1,0},{2,1},{3,2},{4,3},{5,4},{6,5},{7,6},{9,8},{10,9},{11,10},{12... | collective-permute-start | bytes 49160 | tf_op jit(solution)/shard_map/ppermute | solution.py:330
  26.2 5.1 %collective-permute-start.4 = (f32[32,128]{1,0:T(8,128)S(1)}, f32[32,128]{1,0:T(8,128)S(1)}, u32[]{:S(2)}, u32[]{:S(2)}) collective-permute-start(f32[32,128]{1,0:T(8,128)S(1)} %get-tuple-element.34), channel_id=1, source_target_pairs={{0,1},{1,2},{2,3},{3,4},{4,5},{5,6},{6,7},{8,9},{9,10},{10,11},{11... | collective-permute-start | bytes 49160 | tf_op jit(solution)/shard_map/ppermute | solution.py:329

commit v5 on v4

--- a/solution.py
+++ b/solution.py
@@ -213,6 +213,9 @@
     own_ref, own_row, own_col, top_first, bottom_first, top_mid, bottom_mid, half_ref, top_second, bottom_second, final_ref,
     out_ref, a_ref, b_ref, row_ref, col_ref, west_ref,
 ):
+    def put(ref, g, block):
+        ref[:, PAD + 8 * g : PAD + 8 * g + 8, :] = block
+
     for ref in (a_ref, b_ref, row_ref):
         ref[:, :PAD, :] = jnp.zeros((COLUMNS, PAD, LANES), F32)
         ref[:, PAD + TALL :, :] = jnp.zeros((COLUMNS, PAD, LANES), F32)
@@ -225,12 +228,10 @@
         here, there = slice(PAD + begin, PAD + end), slice(PAD + HALO + begin, PAD + HALO + end)
         row_ref[:, there, :] = own_row[:, here, :]
         col_ref[:, there, :] = own_col[:, here, :]
-        a_ref[:, there, :] = own_ref[:, here, :]
+    for g in (0, 7):
+        put(a_ref, g + 2, group(own_ref, g))
     lay_west(col_ref, west_ref, slice(PAD, PAD + 32))
     lay_west(col_ref, west_ref, slice(PAD + 56, PAD + TALL))
-
-    def put(ref, g, block):
-        ref[:, PAD + 8 * g : PAD + 8 * g + 8, :] = block
 
     def several(outer, top_ref, bottom_ref, count):
         def two(i, carry):
@@ -243,8 +244,6 @@
 
         lax.fori_loop(0, count // 2, two, 0)
 
-    b_ref[:, PAD : PAD + 40, :] = a_ref[:, PAD : PAD + 40, :]
-    b_ref[:, PAD + 56 : PAD + TALL, :] = a_ref[:, PAD + 56 : PAD + TALL, :]
     several(0, top_first, bottom_first, EARLY)
     several(0, top_mid, bottom_mid, SWEEPS - EARLY)
     put(a_ref, 3, half_ref[0])

time: 72.5 us -> 72.5 us (level)
  the two profiles are of different devices: /device:TPU:80 before, /device:TPU:72 now
where the time goes in v5:
time: 72.5 us; the launch traced here: 72.1 us
  blocking collectives  36.8 us (51%)
  starting transfers between devices  21.6 us (30%)
  Pallas kernels  9.5 us (13%)
  waiting for transfers between devices  3.38 us (5%)
    all_gather x1, blocking collectives, local(): lax.all_gather(mine, 'mem', axis_index_groups=[[0, 4], [1, 5], [2, 6], [3...  18.4 us
    all_to_all x1, blocking collectives, local(): lax.all_to_all(partial, 'mem', 0, 0, axis_index_groups=along_x, tiled=True)  10.1 us
    ppermute x1, starting transfers between devices, local(): below = lax.ppermute(first, 'tile', up)  8.98 us
    all_to_all x1, blocking collectives, local(): lax.all_to_all(both, 'mem', 0, 0, axis_index_groups=along_x, tiled=True)  8.36 us
    ppermute x1, starting transfers between devices, local(): right = lax.ppermute(first_own, 'tile', leftward)  3.64 us
    pallas_call x1, Pallas kernels, local(): pl.pallas_call(localize, out_shape=f32(4, 32, 256), in_specs=[vmem] * 16,...  3.29 us
    ppermute x1, starting transfers between devices, local(): right = lax.ppermute(first, 'tile', leftward)  2.79 us
    ppermute x1, starting transfers between devices, local(): left = lax.ppermute(last, 'tile', rightward)  2.21 us
  transfers between devices with their start and end apart: 6, of which 3 were waited for; matrix products, arithmetic and copies ran while one was open for 0% of the time, Pallas kernels for 7%

profile of v5, /device:TPU:72, one launch (start us, length us, event | category | flops | bytes accessed | tf_op | source)
XLA Modules:
  0.0 72.1 jit_solution(6423475196212276997)
XLA Ops:
  0.0 0.9 %shard_map.55 = (f32[6,16,256]{2,1,0:T(8,128)S(1)}, f32[6,16,256]{2,1,0:T(8,128)S(1)}) custom-call(f32[2,1,64,256]{3,2,1,0:T(8,128)} %vec_hbm.3, bf16[2,2,1,64,256]{4,3,2,1,0:T(8,128)(2,1)} %ens_hbm.3, f32[2,1,64,256]{3,2,1,0:T(8,128)} %dif_hbm.3, f32[1,64,256]{2,1,0:T(8,128)} %weight_hbm.3), custom_call_target="tpu_custom_call" | custom-call | tf_op jit(solution)/shard_map/pallas_call | solution.py:287
  1.0 9.0 %collective-permute-start.1 = (f32[6,16,256]{2,1,0:T(8,128)S(1)}, f32[6,16,256]{2,1,0:T(8,128)S(1)}, u32[]{:S(2)}, u32[]{:S(2)}) collective-permute-start(f32[6,16,256]{2,1,0:T(8,128)S(1)} %get-tuple-element.27.sent_hbm), channel_id=1, source_target_pairs={{8,0},{9,1},{10,2},{11,3},{12,4},{13,5},{14,6},{15,7},{16,8},{17,9... | collective-permute-start | bytes 294920 | tf_op jit(solution)/shard_map/ppermute | solution.py:295
  9.9 2.0 %collective-permute-start = (f32[6,16,256]{2,1,0:T(8,128)S(1)}, f32[6,16,256]{2,1,0:T(8,128)S(1)}, u32[]{:S(2)}, u32[]{:S(2)}) collective-permute-start(f32[6,16,256]{2,1,0:T(8,128)S(1)} %get-tuple-element.29), channel_id=1, source_target_pairs={{0,8},{1,9},{2,10},{3,11},{4,12},{5,13},{6,14},{7,15},{8,16},{9,17... | collective-permute-start | bytes 294920 | tf_op jit(solution)/shard_map/ppermute | solution.py:294
  12.0 1.4 %shard_map.56 = (f32[6,64,256]{2,1,0:T(8,128)S(1)}, f32[4,64,256]{2,1,0:T(8,128)S(1)}, f32[2,64,256]{2,1,0:T(8,128)S(1)}, f32[64,128]{1,0:T(8,128)S(1)}, f32[64,128]{1,0:T(8,128)S(1)}) custom-call(f32[2,1,64,256]{3,2,1,0:T(8,128)} %vec_hbm.3, bf16[2,2,1,64,256]{4,3,2,1,0:T(8,128)(2,1)} %ens_hbm.3, f32[2,1,64,256]{3,2,1,0:T(8,128)} %dif_hbm.3, ...), custom_call_target="tpu_custom_call" | custom-call | flops 2000000 | bytes 2000000 | tf_op jit(solution)/shard_map/pallas_call | solution.py:297
  13.4 1.9 %collective-permute-start.2 = (f32[64,128]{1,0:T(8,128)S(1)}, f32[64,128]{1,0:T(8,128)S(1)}, u32[]{:S(2)}, u32[]{:S(2)}) collective-permute-start(f32[64,128]{1,0:T(8,128)S(1)} %get-tuple-element.31), channel_id=1, source_target_pairs={{0,1},{1,2},{2,3},{3,4},{4,5},{5,6},{6,7},{8,9},{9,10},{10,11},{11... | collective-permute-start | bytes 98312 | tf_op jit(solution)/shard_map/ppermute | solution.py:308
  15.3 3.6 %collective-permute-start.3 = (f32[64,128]{1,0:T(8,128)S(1)}, f32[64,128]{1,0:T(8,128)S(1)}, u32[]{:S(2)}, u32[]{:S(2)}) collective-permute-start(f32[64,128]{1,0:T(8,128)S(1)} %get-tuple-element.32), channel_id=1, source_target_pairs={{1,0},{2,1},{3,2},{4,3},{5,4},{6,5},{7,6},{9,8},{10,9},{11,10},{12... | collective-permute-start | bytes 98312 | tf_op jit(solution)/shard_map/ppermute | solution.py:309
  18.9 0.0 collective-permute-done.2.left_ref
  19.0 1.6 %collective-permute-done.3.right_ref = f32[64,128]{1,0:T(8,128)S(1)} collective-permute-done((f32[64,128]{1,0:T(8,128)S(1)}, f32[64,128]{1,0:T(8,128)S(1)}, u32[]{:S(2)}, u32[]{:S(2)}) %collective-permute-start.3) | collective-permute-done | bytes 32800 | tf_op jit(solution)/shard_map/ppermute | solution.py:309
  20.5 1.6 %shard_map.57 = (f32[9,80,128]{2,1,0:T(8,128)S(1)}, f32[9,80,128]{2,1,0:T(8,128)S(1)}, f32[9,80,128]{2,1,0:T(8,128)S(1)}, f32[9,80,128]{2,1,0:T(8,128)S(1)}, f32...) custom-call(f32[6,64,256]{2,1,0:T(8,128)S(1)} %get-tuple-element.30.own_ref, ...), custom_call_target="tpu_custom_call" | custom-call | flops 5000000 | bytes 4000000 | tf_op jit(solution)/shard_map/pallas_call | solution.py:315
  22.1 0.0 collective-permute-done.1.below_ref
  22.1 1.2 %collective-permute-done.above_ref = f32[6,16,256]{2,1,0:T(8,128)S(1)} collective-permute-done((f32[6,16,256]{2,1,0:T(8,128)S(1)}, f32[6,16,256]{2,1,0:T(8,128)S(1)}, u32[]{:S(2)}, u32[]{:S(2)}) %collective-permute-start) | collective-permute-done | bytes 98336 | tf_op jit(solution)/shard_map/ppermute | solution.py:294
  23.3 0.1 shard_map.58
  23.4 2.8 %collective-permute-start.5 = (f32[32,128]{1,0:T(8,128)S(1)}, f32[32,128]{1,0:T(8,128)S(1)}, u32[]{:S(2)}, u32[]{:S(2)}) collective-permute-start(f32[32,128]{1,0:T(8,128)S(1)} %get-tuple-element.35.sent_ref), channel_id=1, source_target_pairs={{1,0},{2,1},{3,2},{4,3},{5,4},{6,5},{7,6},{9,8},{10,9},{11,10},{12... | collective-permute-start | bytes 49160 | tf_op jit(solution)/shard_map/ppermute | solution.py:329
  26.2 2.2 %collective-permute-start.4 = (f32[32,128]{1,0:T(8,128)S(1)}, f32[32,128]{1,0:T(8,128)S(1)}, u32[]{:S(2)}, u32[]{:S(2)}) collective-permute-start(f32[32,128]{1,0:T(8,128)S(1)} %get-tuple-element.34), channel_id=1, source_target_pairs={{0,1},{1,2},{2,3},{3,4},{4,5},{5,6},{6,7},{8,9},{9,10},{10,11},{11... | collective-permute-start | bytes 49160 | tf_op jit(solution)/shard_map/ppermute | solution.py:328
  28.4 2.2 %shard_map.59 = (f32[4,9,8,128]{3,2,1,0:T(8,128)S(1)}, f32[4,9,8,128]{3,2,1,0:T(8,128)S(1)}, f32[2,9,8,128]{3,2,1,0:T(8,128)S(1)}, f32[8,9,8,128]{3,2,1,0:T(8,12...) custom-call(f32[9,80,128]{2,1,0:T(8,128)S(1)} %get-tuple-element.33.sent_ref.quarter_ref, ...), custom_call_target="tpu_custom_call" | custom-call | flops 5000000 | bytes 4000000 | tf_op jit(solution)/shard_map/pallas_call | solution.py:330
  30.6 0.0 collective-permute-done.5.right_ref
  30.6 0.6 collective-permute-done.4.left_ref
  31.3 3.3 %shard_map.60 = f32[4,32,256]{2,1,0:T(8,128)S(1)} custom-call(f32[4,64,256]{2,1,0:T(8,128)S(1)} %get-tuple-element.28.scale_ref, f32[6,16,256]{2,1,0:T(8,128)S(1)} %collective-permute-done.above_ref, f32[6,16,256]{2,1,0:T(8,128)S(1)} %collective-permute-done.1.below_ref, f32[32,128]{1,0:T(8,128)S(1)} %collective-permute-done.4.left_ref, ...), custom_call_target="tpu_custom_call" | custom-call | tf_op jit(solution)/shard_map/pallas_call | solution.py:339
  34.6 10.1 %all_to_all.10 = f32[4,32,256]{2,1,0:T(8,128)S(1)} all-to-all(f32[4,32,256]{2,1,0:T(8,128)S(1)} %shard_map.60), channel_id=1, replica_groups={{0,64,128,192},{256,320,384,448},{1,65,129,193},{257,321,385,449},{2,66..., dimensions={0} | all-to-all | bytes 262144 | tf_op jit(solution)/shard_map/all_to_all | solution.py:351
  44.7 18.4 %all-gather = f32[64,256]{1,0:T(8,128)S(1)} all-gather(f32[32,256]{1,0:T(8,128)S(1)} %reduce_sum.9), channel_id=2, replica_groups={{0,256},{64,320},{128,384},{192,448},{1,257},{65,321},{129,385},{193,44..., dimensions={0}, use_global_device_ids=true | all-gather | bytes 98304 | tf_op jit(solution)/shard_map/all_gather | solution.py:353
  63.0 8.4 %all_to_all.11 = f32[4,32,256]{2,1,0:T(8,128)S(1)} all-to-all(f32[4,32,256]{2,1,0:T(8,128)S(1)} %broadcast_in_dim.12), channel_id=1, replica_groups={{0,64,128,192},{256,320,384,448},{1,65,129,193},{257,321,385,449},{2,66..., dimensions={0} | all-to-all | bytes 262144 | tf_op jit(solution)/shard_map/all_to_all | solution.py:355
  71.4 0.7 fusion
  (4 shorter events, 0.0 us)
Async XLA Ops:
  1.0 21.2 %collective-permute-start.1 = (f32[6,16,256]{2,1,0:T(8,128)S(1)}, f32[6,16,256]{2,1,0:T(8,128)S(1)}, u32[]{:S(2)}, u32[]{:S(2)}) collective-permute-start(f32[6,16,256]{2,1,0:T(8,128)S(1)} %get-tuple-element.27.sent_hbm), channel_id=1, source_target_pairs={{8,0},{9,1},{10,2},{11,3},{12,4},{13,5},{14,6},{15,7},{16,8},{17,9... | collective-permute-start | bytes 294920 | tf_op jit(solution)/shard_map/ppermute | solution.py:295
  9.9 13.4 %collective-permute-start = (f32[6,16,256]{2,1,0:T(8,128)S(1)}, f32[6,16,256]{2,1,0:T(8,128)S(1)}, u32[]{:S(2)}, u32[]{:S(2)}) collective-permute-start(f32[6,16,256]{2,1,0:T(8,128)S(1)} %get-tuple-element.29), channel_id=1, source_target_pairs={{0,8},{1,9},{2,10},{3,11},{4,12},{5,13},{6,14},{7,15},{8,16},{9,17... | collective-permute-start | bytes 294920 | tf_op jit(solution)/shard_map/ppermute | solution.py:294
  13.4 5.6 %collective-permute-start.2 = (f32[64,128]{1,0:T(8,128)S(1)}, f32[64,128]{1,0:T(8,128)S(1)}, u32[]{:S(2)}, u32[]{:S(2)}) collective-permute-start(f32[64,128]{1,0:T(8,128)S(1)} %get-tuple-element.31), channel_id=1, source_target_pairs={{0,1},{1,2},{2,3},{3,4},{4,5},{5,6},{6,7},{8,9},{9,10},{10,11},{11... | collective-permute-start | bytes 98312 | tf_op jit(solution)/shard_map/ppermute | solution.py:308
  15.3 5.2 %collective-permute-start.3 = (f32[64,128]{1,0:T(8,128)S(1)}, f32[64,128]{1,0:T(8,128)S(1)}, u32[]{:S(2)}, u32[]{:S(2)}) collective-permute-start(f32[64,128]{1,0:T(8,128)S(1)} %get-tuple-element.32), channel_id=1, source_target_pairs={{1,0},{2,1},{3,2},{4,3},{5,4},{6,5},{7,6},{9,8},{10,9},{11,10},{12... | collective-permute-start | bytes 98312 | tf_op jit(solution)/shard_map/ppermute | solution.py:309
  23.4 7.2 %collective-permute-start.5 = (f32[32,128]{1,0:T(8,128)S(1)}, f32[32,128]{1,0:T(8,128)S(1)}, u32[]{:S(2)}, u32[]{:S(2)}) collective-permute-start(f32[32,128]{1,0:T(8,128)S(1)} %get-tuple-element.35.sent_ref), channel_id=1, source_target_pairs={{1,0},{2,1},{3,2},{4,3},{5,4},{6,5},{7,6},{9,8},{10,9},{11,10},{12... | collective-permute-start | bytes 49160 | tf_op jit(solution)/shard_map/ppermute | solution.py:329
  26.2 5.1 %collective-permute-start.4 = (f32[32,128]{1,0:T(8,128)S(1)}, f32[32,128]{1,0:T(8,128)S(1)}, u32[]{:S(2)}, u32[]{:S(2)}) collective-permute-start(f32[32,128]{1,0:T(8,128)S(1)} %get-tuple-element.34), channel_id=1, source_target_pairs={{0,1},{1,2},{2,3},{3,4},{4,5},{5,6},{6,7},{8,9},{9,10},{10,11},{11... | collective-permute-start | bytes 49160 | tf_op jit(solution)/shard_map/ppermute | solution.py:328
